TPU v7x, 512 devices: a whole 4x4x16 slice. The times are simulated.
512 devices in a mesh: segment: 8 (over x, core), seq: 64 (over z, y).
Axes of the slice: x: 4, y: 4, z: 16, core: 2. Of those that a mesh axis runs over, the one named last changes fastest.
Arguments:
- cotangent: bfloat16 [8, 8192, 4096], P('segment', 'seq'), may hold values from -6 to 6
- gates: bfloat16 [8, 2, 8192, 4096], P('segment', None, 'seq'), may hold values from -6 to 6
- short_weight: float32 [8, 2, 7, 4096], P('segment'), may hold values from -1 to 1
- decay_rates: float32 [8, 2, 4096, 16], P('segment', None, 'seq'), may hold values from 3.6621094e-05 to 0.0333333333
- residues: float32 [8, 2, 4096, 16], P('segment', None, 'seq'), may hold values from -1 to 1
Outputs:
- grad_out: bfloat16 [8, 8192, 4096], P('segment', 'seq')
All inputs are finite; a program needn't handle non-finite values.
Results may differ from a plain program's by a relative error of at most 0.0061.
Values may be sent and summed in bfloat16 or wider, within the bound.
No kernel may reach another device: no remote copies, remote signals or barrier semaphores. Data moves between devices by JAX's collectives and lax.ppermute only.
A program may use at most 128 MiB of HBM per device.

v0:
```python
import jax
import jax.numpy as jnp
import numpy as np
from jax import lax
from jax.experimental import pallas as pl
from jax.experimental.pallas import tpu as pltpu
from jax.sharding import PartitionSpec as P

MODES = 16
SHORT = 7
NODES = 8
HALF = NODES // 2
RATE_LOW, RATE_HIGH = 3.66e-5, 0.0333334
TILE = 512
VMEM_MIB = 44
BF = jnp.bfloat16
F32 = jnp.float32


def cheb(low, high):
    k = np.arange(NODES)
    x = np.cos(np.pi * (2 * k + 1) / (2 * NODES))
    return 0.5 * (low + high) + 0.5 * (high - low) * x


def cardinal(nodes, points):
    rates = cheb(RATE_LOW, RATE_HIGH)
    points = np.asarray(points, np.float64)
    left = np.exp(-np.outer(rates, nodes)).astype(np.longdouble)
    right = np.exp(-np.outer(rates, points.ravel())).astype(np.longdouble)
    for i in range(len(nodes)):
        pivot = i + int(np.argmax(np.abs(left[i:, i])))
        left[[i, pivot]], right[[i, pivot]] = left[[pivot, i]], right[[pivot, i]]
        right[i] /= left[i, i]
        left[i] /= left[i, i]
        for k in range(len(nodes)):
            if k != i:
                right[k] -= left[k, i] * right[i]
                left[k] -= left[k, i] * left[i]
    return right.astype(np.float64).reshape((len(nodes),) + points.shape)


def split_pair(matrix):
    high = matrix.astype(jnp.bfloat16)
    low = (matrix - high.astype(np.float64)).astype(jnp.bfloat16)
    return np.concatenate([high, low], axis=1)


def constants(rows):
    source = cheb(0.0, rows - 1.0)
    target = cheb(0.0, rows + SHORT - 2.0)
    lags = cheb(2.0 - SHORT, rows - 1.0)
    moment = np.zeros((16, rows))
    basis = cardinal(source, np.arange(rows))
    moment[:HALF] = basis[:HALF]
    moment[8 : 8 + HALF] = basis[HALF:]
    spread = np.zeros((rows + 8, 16))
    basis = cardinal(target, np.arange(rows + SHORT - 1)).T
    for part in range(0, 8, HALF):
        spread[: rows + SHORT - 1, part : part + HALF] = basis[:, :HALF]
        spread[: rows + SHORT - 1, 8 + part : 8 + part + HALF] = basis[:, HALF:]
    place = np.arange(rows)
    lag = place[None, :] - place[:, None]
    inside = cardinal(lags, lag) * (lag >= 0)[None]
    place = np.arange(16)
    lag = place[None, :] - place[:8, None]
    live = (lag < 0) & (place[:8, None] < SHORT - 1)
    beyond = -cardinal(lags, np.where(live, lag, 0)) * live[None]
    wide = np.zeros((NODES * 8 + 16 + rows + 8, 2 * rows), jnp.bfloat16)
    wide[: NODES * 8, :32] = split_pair(beyond.reshape(NODES * 8, 16))
    wide[NODES * 8 : NODES * 8 + 16] = split_pair(moment)
    wide[NODES * 8 + 16 :, :32] = split_pair(spread)
    matrices = np.concatenate([split_pair(inside.reshape(NODES * rows, rows)), wide], axis=0)
    return source, rows - target, lags, matrices


def doubled(x):
    return jnp.concatenate([x, x], axis=1)


def low_lanes():
    return lax.broadcasted_iota(jnp.int32, (8, 128), 1) < 64


def top_rows():
    return lax.broadcasted_iota(jnp.int32, (8, 128), 0) < HALF


def packed_rows(values):
    row = lax.broadcasted_iota(jnp.int32, (8, 128), 0) % HALF
    low = low_lanes()
    out = jnp.zeros((8, 128), F32)
    for r in range(HALF):
        out = jnp.where(row == r, jnp.where(low, F32(values[r]), F32(values[r + HALF])), out)
    return out


def unpack(first, second, low):
    return (
        jnp.where(low, first, pltpu.roll(second, 64, 1)),
        jnp.where(low, pltpu.roll(first, 64, 1), second),
    )


def filter_nodes(rate, res, lags):
    rate, res = doubled(rate), doubled(res)
    place = packed_rows(lags)
    total = jnp.zeros((8, 128), F32)
    for m in range(MODES):
        total = total + res[m : m + 1] * jnp.exp(-rate[m : m + 1] * place)
    return total


def twice(x):
    return jnp.concatenate([x, x], axis=0)


class Rows:
    def __init__(self, rows):
        self.inside = slice(0, NODES * rows)
        self.beyond = slice(NODES * rows, NODES * rows + NODES * 8)
        self.moment = slice(self.beyond.stop, self.beyond.stop + 16)
        self.spread = slice(self.moment.stop, self.moment.stop + rows + 8)


def send_moments(product, matrix, fill, at, pay_ref):
    low, top = low_lanes(), top_rows()
    moments = jnp.dot(matrix, twice(product), preferred_element_type=F32)
    for t in range(product.shape[1] // 128):
        columns = slice(t * 128, t * 128 + 128)
        first, second = unpack(moments[0:8, columns], moments[8:16, columns], low)
        block = jnp.concatenate([jnp.where(top, first, fill), jnp.where(top, second, fill)], axis=0)
        pay_ref[at // 8 + t * 16 : at // 8 + t * 16 + 16, :] = block.astype(BF)


def tiles(channels):
    return [(at, slice(at, at + TILE)) for at in range(0, channels, TILE)]


def first_kernel(lags, g_ref, gate_ref, rate_ref, res_ref, matrix_ref, pay_ref, halo_ref, next_ref):
    where = Rows(g_ref.shape[0])
    next_ref[...] = jnp.concatenate([rate_ref[1], res_ref[1]], axis=0)
    taps = filter_nodes(rate_ref[0], res_ref[0], lags)
    matrix = matrix_ref[where.moment, :]
    for at, cut in tiles(g_ref.shape[1]):
        product = (gate_ref[0, :, cut].astype(F32) * g_ref[:, cut].astype(F32)).astype(BF)
        halo_ref[:, cut] = product[:16]
        send_moments(product, matrix, taps, at, pay_ref)


def scan_body(source, gaps, rows, rate, res, pay_ref, out_ref):
    low, top = low_lanes(), top_rows()
    pairs = pay_ref.shape[0] // 16
    rate, res = doubled(rate), doubled(res)
    enter = []
    for r in range(HALF):
        place = jnp.where(low, F32(source[r]), F32(source[r + HALF]))
        enter.append([jnp.exp(-rate[8 * o : 8 * o + 8] * place) for o in range(2)])
    step = [jnp.exp(-rate[8 * o : 8 * o + 8] * F32(rows)) for o in range(2)]
    gap = packed_rows(gaps)
    leave = [res[m : m + 1] * jnp.exp(-rate[m : m + 1] * gap) for m in range(MODES)]

    def one(block, state):
        total = jnp.zeros((8, 128), F32)
        for m in range(MODES):
            total = total + leave[m] * state[m // 8][m % 8 : m % 8 + 1]
        high = total.astype(BF).astype(F32)
        total = jnp.where(top, high, total - high)
        sums = [None, None]
        for o in range(2):
            part = enter[0][o] * block[0:1]
            for r in range(1, HALF):
                part = part + enter[r][o] * block[r : r + 1]
            sums[o] = part + pltpu.roll(part, 64, 1)
        return total, tuple(step[o] * state[o] + sums[o] for o in range(2))

    def pair(i, state):
        place = pl.ds(pl.multiple_of((pairs - 1 - i) * 16, 16), 16)
        blocks = pay_ref[place, :].astype(F32)
        later, state = one(blocks[8:], state)
        earlier, state = one(blocks[:8], state)
        out_ref[place, :] = jnp.concatenate([earlier, later], axis=0).astype(BF)
        return state

    zero = jnp.zeros((8, 128), F32)
    lax.fori_loop(0, pairs, pair, (zero, zero), unroll=4)


def scan_first_kernel(source, gaps, lags, rows, pay_ref, rate_ref, res_ref, next_ref, out_ref, taps_ref):
    scan_body(source, gaps, rows, rate_ref[0], res_ref[0], pay_ref, out_ref)
    taps_ref[...] = filter_nodes(next_ref[:MODES], next_ref[MODES:], lags)


def scan_last_kernel(source, gaps, rows, pay_ref, next_ref, out_ref):
    scan_body(source, gaps, rows, next_ref[:MODES], next_ref[MODES:], pay_ref, out_ref)


def inside_kernel(g_ref, gate_ref, halo_ref, pay_ref, matrix_ref, local_ref, rim_ref):
    rows, channels = g_ref.shape
    where = Rows(rows)
    low = low_lanes()
    for at, cut in tiles(channels):
        product = (gate_ref[0, :, cut].astype(F32) * g_ref[:, cut].astype(F32)).astype(BF)
        parts = []
        for t in range(at // 128, (at + TILE) // 128):
            both = pay_ref[t * 16 : t * 16 + 16, :].astype(F32)
            parts.append(unpack(both[:8], both[8:], low))
        taps = [jnp.concatenate([part[h] for part in parts], axis=1) for h in range(2)]
        waves = jnp.dot(matrix_ref[where.inside, :], twice(product), preferred_element_type=F32)
        edges = jnp.dot(matrix_ref[where.beyond, :32], twice(halo_ref[:, cut]), preferred_element_type=F32)
        local = None
        rim = None
        for n in range(NODES):
            tap = taps[n // HALF][HALF + n % HALF : HALF + n % HALF + 1]
            wave = tap * waves[n * rows : (n + 1) * rows]
            edge = tap * edges[n * 8 : (n + 1) * 8]
            local = wave if local is None else local + wave
            rim = edge if rim is None else rim + edge
        local_ref[:, cut] = local
        rim_ref[:, cut] = rim


def updated_tile(at, cut, g_ref, local_ref, rim_ref, pay_ref, matrix, short):
    rows = g_ref.shape[0]
    low = low_lanes()
    parts = []
    for t in range(at // 128, (at + TILE) // 128):
        both = pay_ref[t * 16 : t * 16 + 16, :].astype(F32)
        parts.append(jnp.concatenate(unpack(both[:8], both[8:], low), axis=0))
    nodes = jnp.concatenate(parts, axis=1).astype(BF)
    outside = jnp.dot(matrix, twice(nodes), preferred_element_type=F32)
    carried = (local_ref[:, cut] + outside[:rows]).astype(BF).astype(F32)
    rim = (rim_ref[:, cut] + outside[rows:]).astype(BF).astype(F32)
    extended = jnp.concatenate([carried, rim], axis=0)
    tail = None
    for j in range(SHORT):
        term = short[j : j + 1] * extended[j : j + rows]
        tail = term if tail is None else tail + term
    return (g_ref[:, cut].astype(F32) + tail).astype(BF)


def turn_kernel(g_ref, local_ref, rim_ref, nodes_ref, short_ref, gate_ref, matrix_ref, new_ref, pay_ref, halo_ref):
    where = Rows(g_ref.shape[0])
    spread = matrix_ref[where.spread, :32]
    moment = matrix_ref[where.moment, :]
    none = jnp.zeros((8, 128), F32)
    for at, cut in tiles(g_ref.shape[1]):
        new = updated_tile(at, cut, g_ref, local_ref, rim_ref, nodes_ref, spread, short_ref[0, :, cut])
        new_ref[:, cut] = new
        product = (gate_ref[0, :, cut].astype(F32) * new.astype(F32)).astype(BF)
        halo_ref[:, cut] = product[:16]
        send_moments(product, moment, none, at, pay_ref)


def merge_kernel(pay_ref, taps_ref, g_ref, out_ref, same_ref):
    top = top_rows()
    taps = taps_ref[...]
    for t in range(0, pay_ref.shape[0], 16):
        both = pay_ref[t : t + 16, :].astype(F32)
        block = jnp.concatenate([jnp.where(top, both[:8], taps), jnp.where(top, both[8:], taps)], axis=0)
        out_ref[t : t + 16, :] = block.astype(BF)


def last_kernel(g_ref, local_ref, rim_ref, nodes_ref, short_ref, matrix_ref, out_ref):
    spread = matrix_ref[Rows(g_ref.shape[0]).spread, :32]
    for at, cut in tiles(g_ref.shape[1]):
        out_ref[:, cut] = updated_tile(at, cut, g_ref, local_ref, rim_ref, nodes_ref, spread, short_ref[0, :, cut])


PARAMS = pltpu.CompilerParams(vmem_limit_bytes=VMEM_MIB * 1024 * 1024)


def call(kernel, name, ins, outs, fixed=(), layer=0, specs=None, out_specs=None, aliases=None, flops=0):
    def whole(array):
        return pl.BlockSpec(array.shape, lambda i: (0,) * len(array.shape))

    return pl.pallas_call(
        lambda *refs: kernel(*fixed, *refs),
        grid=(1,),
        in_specs=[(specs or {}).get(k) or whole(x) for k, x in enumerate(ins)],
        out_specs=[(out_specs or {}).get(k) or whole(x) for k, x in enumerate(outs)],
        out_shape=list(outs),
        input_output_aliases=aliases or {},
        compiler_params=PARAMS,
        cost_estimate=pl.CostEstimate(flops=flops, bytes_accessed=8 * 2**20, transcendentals=0),
        name=name,
    )(*ins)


def on_device(cotangent, gates, short_weight, decay_rates, residues):
    g = cotangent[0]
    gates = gates[0]
    short_weight = short_weight[0]
    rates = jnp.swapaxes(decay_rates[0], 1, 2)
    weights = jnp.swapaxes(residues[0], 1, 2)
    rows, channels = g.shape
    shards = lax.axis_size("seq")
    segments = lax.axis_size("segment")
    source, gaps, lags, matrices = constants(rows)
    matrices = jnp.asarray(matrices)

    def shape(size, dtype):
        return jax.ShapeDtypeStruct(size, dtype)

    def around(x, distance):
        return lax.ppermute(x, "segment", [(i, (i + distance) % segments) for i in range(segments)])

    def across(x):
        x = x.reshape(shards, 8, 128)
        return lax.all_to_all(x, "seq", split_axis=0, concat_axis=0, tiled=True).reshape(shards * 8, 128)

    pay_shape = shape((shards * 8, 128), BF)
    halo_shape = shape((16, channels), BF)
    row_shape = shape((rows, channels), BF)
    local_shapes = [shape((rows, channels), F32), shape((8, channels), F32)]
    layer_gate = pl.BlockSpec((1, rows, channels), lambda i: (0, 0, 0))
    layer_short = pl.BlockSpec((1, SHORT, channels), lambda i: (0, 0, 0))

    pay, halo, params = call(
        first_kernel, "first", [g, gates, rates, weights, matrices],
        [pay_shape, halo_shape, shape((2 * MODES, channels // shards), F32)],
        fixed=(lags,), specs={1: layer_gate},
    )
    late_gates = gates[1:]
    gates_early = around(late_gates, 1)
    gates_late = around(late_gates, -1)
    params_late = around(params, -1)
    short_late = around(short_weight[1:], -1)
    halo = lax.ppermute(halo, "seq", [(i, i - 1) for i in range(1, shards)])
    got = across(pay)
    back, taps = call(
        scan_first_kernel, "scan", [got, rates, weights, params_late],
        [pay_shape, shape((8, 128), F32)], fixed=(source, gaps, lags, rows),
    )
    nodes = across(back)
    local, rim = call(
        inside_kernel, "inside", [g, gates, halo, got, matrices], local_shapes, specs={1: layer_gate},
        flops=2 * NODES * rows * 2 * rows * channels,
    )
    g, pay, halo = call(
        turn_kernel, "turn", [g, local, rim, nodes, short_weight, gates_early, matrices],
        [row_shape, pay_shape, halo_shape], specs={4: layer_short},
    )
    pay = around(pay, -2)
    moves = [
        (s * shards + k, (s - 2) % segments * shards + k - 1) for s in range(segments) for k in range(1, shards)
    ]
    halo = lax.ppermute(halo, ("segment", "seq"), moves)
    anywhere = pl.BlockSpec(memory_space=pl.ANY)
    pay, g = call(
        merge_kernel, "merge", [pay, taps, g], [pay_shape, row_shape],
        specs={2: anywhere}, out_specs={1: anywhere}, aliases={2: 1},
    )
    g = around(g, -2)
    got = across(pay)
    (back,) = call(
        scan_last_kernel, "scan", [got, params_late], [pay_shape], fixed=(source, gaps, rows)
    )
    nodes = across(back)
    local, rim = call(
        inside_kernel, "inside", [g, gates_late, halo, got, matrices], local_shapes,
        flops=2 * NODES * rows * 2 * rows * channels,
    )
    (g,) = call(last_kernel, "last", [g, local, rim, nodes, short_late, matrices], [row_shape])
    return g[None]


def solution(mesh):
    in_specs = (
        P("segment", "seq", None),
        P("segment", None, "seq", None),
        P("segment", None, None, None),
        P("segment", None, "seq", None),
        P("segment", None, "seq", None),
    )
    return jax.shard_map(
        on_device, mesh=mesh, in_specs=in_specs, out_specs=P("segment", "seq", None), check_vma=False
    )
```

profile of v0, /device:TPU:8, one launch (start us, length us, event | category | flops | bytes accessed | tf_op | source)
XLA Modules:
  0.0 146.7 jit_solution(4811579127102297984)
XLA Ops:
  0.0 0.0 copy-start.12
  0.0 2.4 %slice_bitcast_fusion = bf16[1,128,4096]{2,1,0:T(8,128)(2,1)} fusion(bf16[1,2,128,4096]{3,2,1,0:T(8,128)(2,1)} %param.7), kind=kLoop, calls=%fused_computation | loop fusion | bytes 2097152 | tf_op jit(solution)/shard_map/slice | solution.py:324
  2.4 0.0 collective-permute-start.2
  2.4 0.0 copy-done
  2.4 0.0 copy-done.3
  2.4 0.0 copy-done.11
  2.5 0.0 copy-start.1
  2.5 1.6 %copy-done.1 = bf16[1,2,128,4096]{3,2,1,0:T(8,128)(2,1)S(1)} copy-done((bf16[1,2,128,4096]{3,2,1,0:T(8,128)(2,1)S(1)}, bf16[1,2,128,4096]{3,2,1,0:T(8,128)(2,1)}, u32[]{:S(2)}) %copy-start.1) | copy-done | bytes 2097176
  4.1 1.1 first.1
  5.2 18.7 %all-to-all-start = ((bf16[64,8,128]{2,1,0:T(8,128)(2,1)}), bf16[64,8,128]{2,1,0:T(8,128)(2,1)S(1)}, u32[]{:S(2)}, u32[]{:S(2)}) async-start(bf16[64,8,128]{2,1,0:T(8,128)(2,1)} %bitcast.6), calls=%async_computation | async-start | bytes 262144 | tf_op jit(solution)/shard_map/all_to_all | solution.py:310
  23.9 2.4 %collective-permute-start.1 = (f32[32,64]{1,0:T(8,128)S(1)}, f32[32,64]{1,0:T(8,128)S(1)}, u32[]{:S(2)}, u32[]{:S(2)}) collective-permute-start(f32[32,64]{1,0:T(8,128)S(1)} %get-tuple-element.23), channel_id=1, source_target_pairs={{0,448},{64,0},{128,64},{192,128},{256,192},{320,256},{384,320},{4... | collective-permute-start | bytes 24584 | tf_op jit(solution)/shard_map/ppermute | solution.py:306
  26.3 1.4 collective-permute-done.1.refs_3_.refs_1_
  27.8 13.3 %all-to-all-done = bf16[64,8,128]{2,1,0:T(8,128)(2,1)S(1)} async-done(((bf16[64,8,128]{2,1,0:T(8,128)(2,1)}), bf16[64,8,128]{2,1,0:T(8,128)(2,1)S(1)}, u32[]{:S(2)}, u32[]{:S(2)}) %all-to-all-start) | async-done | bytes 131104 | tf_op jit(solution)/shard_map/all_to_all | solution.py:310
  41.1 1.9 %scan.2 = (bf16[512,128]{1,0:T(8,128)(2,1)}, f32[8,128]{1,0:T(8,128)S(1)}) custom-call(bf16[512,128]{1,0:T(8,128)(2,1)S(1)} %bitcast.33, f32[2,16,64]{2,1,0:T(8,128)S(1)} %bitcast.36, f32[2,16,64]{2,1,0:T(8,128)S(1)} %bitcast.38, f32[32,64]{1,0:T(8,128)S(1)} %collective-permute-done.1.refs_3_.refs_1_), custom_call_target="tpu_custom_call" | custom-call | bytes 8388608 | tf_op jit(solution)/shard_map/scan/pallas_call | solution.py:277
  42.9 5.8 %all-to-all-start.1 = ((bf16[64,8,128]{2,1,0:T(8,128)(2,1)}), bf16[64,8,128]{2,1,0:T(8,128)(2,1)S(1)}, u32[]{:S(2)}, u32[]{:S(2)}) async-start(bf16[64,8,128]{2,1,0:T(8,128)(2,1)} %bitcast.10), calls=%async_computation.1 | async-start | bytes 262144 | tf_op jit(solution)/shard_map/all_to_all | solution.py:310
  48.8 2.4 %collective-permute-start = (bf16[16,4096]{1,0:T(8,128)(2,1)S(1)}, bf16[16,4096]{1,0:T(8,128)(2,1)S(1)}, u32[]{:S(2)}, u32[]{:S(2)}) collective-permute-start(bf16[16,4096]{1,0:T(8,128)(2,1)S(1)} %get-tuple-element.19), channel_id=1, source_target_pairs={{1,0},{2,1},{3,2},{4,3},{5,4},{6,5},{7,6},{8,7},{9,8},{10,9},{11,1... | collective-permute-start | bytes 393224 | tf_op jit(solution)/shard_map/ppermute | solution.py:329
  51.2 1.1 copy.12
  52.2 4.3 %collective-permute-done.refs_2_ = bf16[16,4096]{1,0:T(8,128)(2,1)S(1)} collective-permute-done((bf16[16,4096]{1,0:T(8,128)(2,1)S(1)}, bf16[16,4096]{1,0:T(8,128)(2,1)S(1)}, u32[]{:S(2)}, u32[]{:S(2)}) %collective-permute-start) | collective-permute-done | bytes 131104 | tf_op jit(solution)/shard_map/ppermute | solution.py:329
  56.6 1.2 copy-done.4
  57.8 2.8 %inside.2 = (f32[128,4096]{1,0:T(8,128)S(1)}, f32[8,4096]{1,0:T(8,128)S(1)}) custom-call(bf16[128,4096]{1,0:T(8,128)(2,1)S(1)} %bitcast.26, bf16[2,128,4096]{2,1,0:T(8,128)(2,1)S(1)} %bitcast.24, bf16[16,4096]{1,0:T(8,128)(2,1)S(1)} %collective-permute-done.refs_2_, bf16[512,128]{1,0:T(8,128)(2,1)S(1)} %bitcast.34, bf16[1240,256]{1,0:T(8,128)(2,1)S(1)} %copy-done), custom_call_target="tpu_custom_call" | custom-call | flops 2147483648 | bytes 8388608 | tf_op jit(solution)/shard_map/inside/pallas_call | solution.py:277
  60.7 1.3 copy-done.6
  62.0 4.4 %all-to-all-done.1 = bf16[64,8,128]{2,1,0:T(8,128)(2,1)S(1)} async-done(((bf16[64,8,128]{2,1,0:T(8,128)(2,1)}), bf16[64,8,128]{2,1,0:T(8,128)(2,1)S(1)}, u32[]{:S(2)}, u32[]{:S(2)}) %all-to-all-start.1) | async-done | bytes 131104 | tf_op jit(solution)/shard_map/all_to_all | solution.py:310
  66.4 0.0 collective-permute-done.2.refs_5_
  66.4 1.2 copy-done.5
  67.6 1.6 %copy-done.7 = f32[128,4096]{1,0:T(8,128)S(1)} copy-done((f32[128,4096]{1,0:T(8,128)S(1)}, f32[128,4096]{1,0:T(8,128)}, u32[]{:S(2)}) %copy-start.7) | copy-done | bytes 2097176
  69.2 5.3 %turn.1 = (bf16[128,4096]{1,0:T(8,128)(2,1)S(1)}, bf16[512,128]{1,0:T(8,128)(2,1)S(1)}, bf16[16,4096]{1,0:T(8,128)(2,1)S(1)}) custom-call(bf16[128,4096]{1,0:T(8,128)(2,1)S(1)} %bitcast.27, f32[128,4096]{1,0:T(8,128)S(1)} %copy-done.7, f32[8,4096]{1,0:T(8,128)S(1)} %get-tuple-element.22.refs_2_, bf16[512,128]{1,0:T(8,128)(2,1)S(1)} %bitcast.30, ...), custom_call_target="tpu_custom_call" | custom-call | bytes 8388608 | tf_op jit(solution)/shard_map/turn/pallas_call | solution.py:277
  74.5 2.9 %collective-permute-start.3 = (bf16[512,128]{1,0:T(8,128)(2,1)S(1)}, bf16[512,128]{1,0:T(8,128)(2,1)S(1)}, u32[]{:S(2)}, u32[]{:S(2)}) collective-permute-start(bf16[512,128]{1,0:T(8,128)(2,1)S(1)} %get-tuple-element.25), channel_id=1, source_target_pairs={{0,384},{64,448},{128,0},{192,64},{256,128},{320,192},{384,256},{4... | collective-permute-start | bytes 393224 | tf_op jit(solution)/shard_map/ppermute | solution.py:306
  77.4 3.9 %collective-permute-done.3.refs_0_ = bf16[512,128]{1,0:T(8,128)(2,1)S(1)} collective-permute-done((bf16[512,128]{1,0:T(8,128)(2,1)S(1)}, bf16[512,128]{1,0:T(8,128)(2,1)S(1)}, u32[]{:S(2)}, u32[]{:S(2)}) %collective-permute-start.3) | collective-permute-done | bytes 131104 | tf_op jit(solution)/shard_map/ppermute | solution.py:306
  81.3 0.7 merge.1
  82.0 12.9 %all-to-all-start.2 = ((bf16[64,8,128]{2,1,0:T(8,128)(2,1)}), bf16[64,8,128]{2,1,0:T(8,128)(2,1)S(1)}, u32[]{:S(2)}, u32[]{:S(2)}) async-start(bf16[64,8,128]{2,1,0:T(8,128)(2,1)} %bitcast.14), calls=%async_computation.2 | async-start | bytes 262144 | tf_op jit(solution)/shard_map/all_to_all | solution.py:310
  94.9 0.0 collective-permute-start.5
  95.0 4.6 %collective-permute-start.4 = (bf16[128,4096]{1,0:T(8,128)(2,1)S(1)}, bf16[128,4096]{1,0:T(8,128)(2,1)S(1)}, u32[]{:S(2)}, u32[]{:S(2)}) collective-permute-start(bf16[128,4096]{1,0:T(8,128)(2,1)S(1)} %get-tuple-element.28), channel_id=1, source_target_pairs={{0,384},{64,448},{128,0},{192,64},{256,128},{320,192},{384,256},{4... | collective-permute-start | bytes 3145736 | tf_op jit(solution)/shard_map/ppermute | solution.py:306
  99.6 2.5 %collective-permute-start.6 = (bf16[16,4096]{1,0:T(8,128)(2,1)S(1)}, bf16[16,4096]{1,0:T(8,128)(2,1)S(1)}, u32[]{:S(2)}, u32[]{:S(2)}) collective-permute-start(bf16[16,4096]{1,0:T(8,128)(2,1)S(1)} %get-tuple-element.29), channel_id=1, source_target_pairs={{1,384},{2,385},{3,386},{4,387},{5,388},{6,389},{7,390},{8,391},{9... | collective-permute-start | bytes 393224 | tf_op jit(solution)/shard_map/ppermute | solution.py:348
  102.1 8.8 %all-to-all-done.2 = bf16[64,8,128]{2,1,0:T(8,128)(2,1)S(1)} async-done(((bf16[64,8,128]{2,1,0:T(8,128)(2,1)}), bf16[64,8,128]{2,1,0:T(8,128)(2,1)S(1)}, u32[]{:S(2)}, u32[]{:S(2)}) %all-to-all-start.2) | async-done | bytes 131104 | tf_op jit(solution)/shard_map/all_to_all | solution.py:310
  110.8 1.9 %scan.3 = bf16[512,128]{1,0:T(8,128)(2,1)} custom-call(bf16[512,128]{1,0:T(8,128)(2,1)S(1)} %bitcast.31, f32[32,64]{1,0:T(8,128)S(1)} %collective-permute-done.1.refs_3_.refs_1_), custom_call_target="tpu_custom_call" | custom-call | bytes 8388608 | tf_op jit(solution)/shard_map/scan/pallas_call | solution.py:277
  112.7 6.5 %all-to-all-start.3 = ((bf16[64,8,128]{2,1,0:T(8,128)(2,1)}), bf16[64,8,128]{2,1,0:T(8,128)(2,1)S(1)}, u32[]{:S(2)}, u32[]{:S(2)}) async-start(bf16[64,8,128]{2,1,0:T(8,128)(2,1)} %bitcast.16), calls=%async_computation.3 | async-start | bytes 262144 | tf_op jit(solution)/shard_map/all_to_all | solution.py:310
  119.2 0.0 collective-permute-start.7
  119.2 0.0 collective-permute-done.5.refs_1_
  119.2 16.4 %collective-permute-done.6.refs_2_ = bf16[16,4096]{1,0:T(8,128)(2,1)S(1)} collective-permute-done((bf16[16,4096]{1,0:T(8,128)(2,1)S(1)}, bf16[16,4096]{1,0:T(8,128)(2,1)S(1)}, u32[]{:S(2)}, u32[]{:S(2)}) %collective-permute-start.6) | collective-permute-done | bytes 131104 | tf_op jit(solution)/shard_map/ppermute | solution.py:348
  135.6 0.0 collective-permute-done.4.refs_0_
  135.6 1.0 copy-done.8
  136.6 1.2 copy-done.9
  137.8 4.0 %inside.3 = (f32[128,4096]{1,0:T(8,128)S(1)}, f32[8,4096]{1,0:T(8,128)S(1)}) custom-call(bf16[128,4096]{1,0:T(8,128)(2,1)S(1)} %copy-done.9, bf16[1,128,4096]{2,1,0:T(8,128)(2,1)} %collective-permute-done.5.refs_1_, bf16[16,4096]{1,0:T(8,128)(2,1)S(1)} %collective-permute-done.6.refs_2_, bf16[512,128]{1,0:T(8,128)(2,1)S(1)} %bitcast.32, ...), custom_call_target="tpu_custom_call" | custom-call | flops 2147483648 | bytes 8388608 | tf_op jit(solution)/shard_map/inside/pallas_call | solution.py:277
  141.9 0.0 collective-permute-done.7.refs_4_
  141.9 0.0 all-to-all-done.3
  141.9 0.0 copy-start.10
  141.9 1.2 copy-done.10
  143.1 3.6 %last.1 = bf16[128,4096]{1,0:T(8,128)(2,1)} custom-call(bf16[128,4096]{1,0:T(8,128)(2,1)S(1)} %copy-done.10, f32[128,4096]{1,0:T(8,128)S(1)} %get-tuple-element.31.refs_1_, f32[8,4096]{1,0:T(8,128)S(1)} %get-tuple-element.32.refs_2_, bf16[512,128]{1,0:T(8,128)(2,1)S(1)} %bitcast.29, f32[1,7,4096]{2,1,0:T(8,128)S(1)} %collective-permute-done.7.refs_4_, ...), custom_call_target="tpu_custom_call" | custom-call | bytes 8388608 | tf_op jit(solution)/shard_map/last/pallas_call | solution.py:277
  (13 shorter events, 0.0 us)
Async XLA Ops:
  0.0 2.4 %copy-start = (bf16[1240,256]{1,0:T(8,128)(2,1)S(1)}, bf16[1240,256]{1,0:T(8,128)(2,1)}, u32[]{:S(2)}) copy-start(bf16[1240,256]{1,0:T(8,128)(2,1)} %constant.2.clone.refs_4_.refs_6_.refs_5_) | copy-start | bytes 1904644
  0.0 2.4 %copy-start.3 = (bf16[1,128,4096]{2,1,0:T(8,128)(2,1)S(1)}, bf16[1,128,4096]{2,1,0:T(8,128)(2,1)}, u32[]{:S(2)}) copy-start(bf16[1,128,4096]{2,1,0:T(8,128)(2,1)} %param.6) | copy-start | bytes 3145732
  0.0 2.4 %copy-start.11 = (f32[1,2,64,16]{2,3,1,0:T(8,128)S(1)}, f32[1,2,64,16]{2,3,1,0:T(8,128)}, u32[]{:S(2)}) copy-start(f32[1,2,64,16]{2,3,1,0:T(8,128)} %param.9) | copy-start | bytes 24580
  0.0 2.4 %copy-start.12 = (f32[1,2,64,16]{2,3,1,0:T(8,128)S(1)}, f32[1,2,64,16]{2,3,1,0:T(8,128)}, u32[]{:S(2)}) copy-start(f32[1,2,64,16]{2,3,1,0:T(8,128)} %param.10) | copy-start | bytes 24580
  2.4 63.9 %collective-permute-start.2 = (bf16[1,128,4096]{2,1,0:T(8,128)(2,1)}, bf16[1,128,4096]{2,1,0:T(8,128)(2,1)}, u32[]{:S(2)}, u32[]{:S(2)}) collective-permute-start(bf16[1,128,4096]{2,1,0:T(8,128)(2,1)} %slice_bitcast_fusion), channel_id=1, source_target_pairs={{0,64},{64,128},{128,192},{192,256},{256,320},{320,384},{384,448},... | collective-permute-start | bytes 3145736 | tf_op jit(solution)/shard_map/ppermute | solution.py:306
  2.5 1.6 %copy-start.1 = (bf16[1,2,128,4096]{3,2,1,0:T(8,128)(2,1)S(1)}, bf16[1,2,128,4096]{3,2,1,0:T(8,128)(2,1)}, u32[]{:S(2)}) copy-start(bf16[1,2,128,4096]{3,2,1,0:T(8,128)(2,1)} %param.7) | copy-start | bytes 6291460
  4.1 52.5 %copy-start.2 = (bf16[1,2,128,4096]{3,2,1,0:T(8,128)(2,1)S(1)}, bf16[1,2,128,4096]{3,2,1,0:T(8,128)(2,1)}, u32[]{:S(2)}) copy-start(bf16[1,2,128,4096]{3,2,1,0:T(8,128)(2,1)} %param.7) | copy-start | bytes 6291460
  5.2 35.9 %all-to-all-start = ((bf16[64,8,128]{2,1,0:T(8,128)(2,1)}), bf16[64,8,128]{2,1,0:T(8,128)(2,1)S(1)}, u32[]{:S(2)}, u32[]{:S(2)}) async-start(bf16[64,8,128]{2,1,0:T(8,128)(2,1)} %bitcast.6), calls=%async_computation | async-start | bytes 262144 | tf_op jit(solution)/shard_map/all_to_all | solution.py:310
  23.9 3.8 %collective-permute-start.1 = (f32[32,64]{1,0:T(8,128)S(1)}, f32[32,64]{1,0:T(8,128)S(1)}, u32[]{:S(2)}, u32[]{:S(2)}) collective-permute-start(f32[32,64]{1,0:T(8,128)S(1)} %get-tuple-element.23), channel_id=1, source_target_pairs={{0,448},{64,0},{128,64},{192,128},{256,192},{320,256},{384,320},{4... | collective-permute-start | bytes 24584 | tf_op jit(solution)/shard_map/ppermute | solution.py:306
  42.9 23.4 %all-to-all-start.1 = ((bf16[64,8,128]{2,1,0:T(8,128)(2,1)}), bf16[64,8,128]{2,1,0:T(8,128)(2,1)S(1)}, u32[]{:S(2)}, u32[]{:S(2)}) async-start(bf16[64,8,128]{2,1,0:T(8,128)(2,1)} %bitcast.10), calls=%async_computation.1 | async-start | bytes 262144 | tf_op jit(solution)/shard_map/all_to_all | solution.py:310
  48.8 7.8 %collective-permute-start = (bf16[16,4096]{1,0:T(8,128)(2,1)S(1)}, bf16[16,4096]{1,0:T(8,128)(2,1)S(1)}, u32[]{:S(2)}, u32[]{:S(2)}) collective-permute-start(bf16[16,4096]{1,0:T(8,128)(2,1)S(1)} %get-tuple-element.19), channel_id=1, source_target_pairs={{1,0},{2,1},{3,2},{4,3},{5,4},{6,5},{7,6},{8,7},{9,8},{10,9},{11,1... | collective-permute-start | bytes 393224 | tf_op jit(solution)/shard_map/ppermute | solution.py:329
  56.6 1.2 copy-start.4
  60.6 1.4 copy-start.6
  66.4 1.2 copy-start.5
  67.6 1.6 %copy-start.7 = (f32[128,4096]{1,0:T(8,128)S(1)}, f32[128,4096]{1,0:T(8,128)}, u32[]{:S(2)}) copy-start(f32[128,4096]{1,0:T(8,128)} %copy-done.6) | copy-start | bytes 6291460
  74.5 6.9 %collective-permute-start.3 = (bf16[512,128]{1,0:T(8,128)(2,1)S(1)}, bf16[512,128]{1,0:T(8,128)(2,1)S(1)}, u32[]{:S(2)}, u32[]{:S(2)}) collective-permute-start(bf16[512,128]{1,0:T(8,128)(2,1)S(1)} %get-tuple-element.25), channel_id=1, source_target_pairs={{0,384},{64,448},{128,0},{192,64},{256,128},{320,192},{384,256},{4... | collective-permute-start | bytes 393224 | tf_op jit(solution)/shard_map/ppermute | solution.py:306
  82.0 28.8 %all-to-all-start.2 = ((bf16[64,8,128]{2,1,0:T(8,128)(2,1)}), bf16[64,8,128]{2,1,0:T(8,128)(2,1)S(1)}, u32[]{:S(2)}, u32[]{:S(2)}) async-start(bf16[64,8,128]{2,1,0:T(8,128)(2,1)} %bitcast.14), calls=%async_computation.2 | async-start | bytes 262144 | tf_op jit(solution)/shard_map/all_to_all | solution.py:310
  94.9 24.2 %collective-permute-start.5 = (bf16[1,128,4096]{2,1,0:T(8,128)(2,1)}, bf16[1,128,4096]{2,1,0:T(8,128)(2,1)}, u32[]{:S(2)}, u32[]{:S(2)}) collective-permute-start(bf16[1,128,4096]{2,1,0:T(8,128)(2,1)} %slice_bitcast_fusion), channel_id=1, source_target_pairs={{0,448},{64,0},{128,64},{192,128},{256,192},{320,256},{384,320},{4... | collective-permute-start | bytes 3145736 | tf_op jit(solution)/shard_map/ppermute | solution.py:306
  95.0 40.7 %collective-permute-start.4 = (bf16[128,4096]{1,0:T(8,128)(2,1)S(1)}, bf16[128,4096]{1,0:T(8,128)(2,1)S(1)}, u32[]{:S(2)}, u32[]{:S(2)}) collective-permute-start(bf16[128,4096]{1,0:T(8,128)(2,1)S(1)} %get-tuple-element.28), channel_id=1, source_target_pairs={{0,384},{64,448},{128,0},{192,64},{256,128},{320,192},{384,256},{4... | collective-permute-start | bytes 3145736 | tf_op jit(solution)/shard_map/ppermute | solution.py:306
  99.6 36.1 %collective-permute-start.6 = (bf16[16,4096]{1,0:T(8,128)(2,1)S(1)}, bf16[16,4096]{1,0:T(8,128)(2,1)S(1)}, u32[]{:S(2)}, u32[]{:S(2)}) collective-permute-start(bf16[16,4096]{1,0:T(8,128)(2,1)S(1)} %get-tuple-element.29), channel_id=1, source_target_pairs={{1,384},{2,385},{3,386},{4,387},{5,388},{6,389},{7,390},{8,391},{9... | collective-permute-start | bytes 393224 | tf_op jit(solution)/shard_map/ppermute | solution.py:348
  112.7 29.2 %all-to-all-start.3 = ((bf16[64,8,128]{2,1,0:T(8,128)(2,1)}), bf16[64,8,128]{2,1,0:T(8,128)(2,1)S(1)}, u32[]{:S(2)}, u32[]{:S(2)}) async-start(bf16[64,8,128]{2,1,0:T(8,128)(2,1)} %bitcast.16), calls=%async_computation.3 | async-start | bytes 262144 | tf_op jit(solution)/shard_map/all_to_all | solution.py:310
  119.2 22.7 %collective-permute-start.7 = (f32[1,7,4096]{2,1,0:T(8,128)S(1)}, f32[1,7,4096]{2,1,0:T(8,128)S(1)}, u32[]{:S(2)}, u32[]{:S(2)}) collective-permute-start(f32[1,7,4096]{2,1,0:T(8,128)S(1)} %slice_bitcast_fusion.1), channel_id=1, source_target_pairs={{0,448},{64,0},{128,64},{192,128},{256,192},{320,256},{384,320},{4... | collective-permute-start | bytes 344072 | tf_op jit(solution)/shard_map/ppermute | solution.py:306
  135.6 1.0 copy-start.8
  136.6 1.2 copy-start.9
  141.9 1.2 copy-start.10
where the time goes:
time: 147 us
  starting transfers between devices  58.7 us (40%)
  waiting for transfers between devices  52.6 us (36%)
  Pallas kernels  21.3 us (14%)
  local copies, waits for them, and re-layouts  13.9 us (9%)
    all_to_all x4, starting transfers between devices, across(): lax.all_to_all(x, 'seq', split_axis=0, concat_axis=0, tiled=True)  43.9 us
    all_to_all x4, waiting for transfers between devices, across(): lax.all_to_all(x, 'seq', split_axis=0, concat_axis=0, tiled=True)  26.5 us
    pallas_call x8, Pallas kernels, call(): pl.pallas_call(lambda *refs: kernel(*fixed, *refs), grid=(1,), in_specs=[...  21.3 us
    ppermute x1, waiting for transfers between devices, on_device(): halo = lax.ppermute(halo, ('segment', 'seq'), moves)  16.4 us
    unnamed x27, local copies, waits for them, and re-layouts  11.5 us
    ppermute x6, starting transfers between devices, around(): lax.ppermute(x, 'segment', [(i, (i + distance) % segments) for i in range...  9.97 us
    ppermute x6, waiting for transfers between devices, around(): lax.ppermute(x, 'segment', [(i, (i + distance) % segments) for i in range...  5.36 us
    ppermute x1, waiting for transfers between devices, on_device(): halo = lax.ppermute(halo, 'seq', [(i, i - 1) for i in range(1, shards)])  4.33 us
  transfers between devices with their start and end apart: 12, of which 7 were waited for; matrix products, arithmetic and copies ran while one was open for 1% of the time, Pallas kernels for 8%

commit v1 on v0

--- a/solution.py
+++ b/solution.py
@@ -54,11 +54,8 @@
     basis = cardinal(source, np.arange(rows))
     moment[:HALF] = basis[:HALF]
     moment[8 : 8 + HALF] = basis[HALF:]
-    spread = np.zeros((rows + 8, 16))
-    basis = cardinal(target, np.arange(rows + SHORT - 1)).T
-    for part in range(0, 8, HALF):
-        spread[: rows + SHORT - 1, part : part + HALF] = basis[:, :HALF]
-        spread[: rows + SHORT - 1, 8 + part : 8 + part + HALF] = basis[:, HALF:]
+    spread = np.zeros((rows + 8, NODES))
+    spread[: rows + SHORT - 1] = cardinal(target, np.arange(rows + SHORT - 1)).T
     place = np.arange(rows)
     lag = place[None, :] - place[:, None]
     inside = cardinal(lags, lag) * (lag >= 0)[None]
@@ -69,7 +66,7 @@
     wide = np.zeros((NODES * 8 + 16 + rows + 8, 2 * rows), jnp.bfloat16)
     wide[: NODES * 8, :32] = split_pair(beyond.reshape(NODES * 8, 16))
     wide[NODES * 8 : NODES * 8 + 16] = split_pair(moment)
-    wide[NODES * 8 + 16 :, :32] = split_pair(spread)
+    wide[NODES * 8 + 16 :, : 2 * NODES] = split_pair(spread)
     matrices = np.concatenate([split_pair(inside.reshape(NODES * rows, rows)), wide], axis=0)
     return source, rows - target, lags, matrices
 
@@ -123,34 +120,41 @@
         self.spread = slice(self.moment.stop, self.moment.stop + rows + 8)
 
 
-def send_moments(product, matrix, fill, at, pay_ref):
+def send_moments(product, matrix, taps, at, pay_ref):
     low, top = low_lanes(), top_rows()
     moments = jnp.dot(matrix, twice(product), preferred_element_type=F32)
+    blocks = []
     for t in range(product.shape[1] // 128):
         columns = slice(t * 128, t * 128 + 128)
         first, second = unpack(moments[0:8, columns], moments[8:16, columns], low)
-        block = jnp.concatenate([jnp.where(top, first, fill), jnp.where(top, second, fill)], axis=0)
-        pay_ref[at // 8 + t * 16 : at // 8 + t * 16 + 16, :] = block.astype(BF)
+        if taps is None:
+            blocks.append(jnp.where(top, first, pltpu.roll(second, HALF, 0)))
+        else:
+            blocks += [jnp.where(top, first, taps), jnp.where(top, second, taps)]
+    for k in range(0, len(blocks), 2):
+        start = at // 64 * 8 // (2 if taps is None else 1) + k * 8
+        pay_ref[start : start + 16, :] = jnp.concatenate(blocks[k : k + 2], axis=0).astype(BF)
 
 
 def tiles(channels):
     return [(at, slice(at, at + TILE)) for at in range(0, channels, TILE)]
 
 
-def first_kernel(lags, g_ref, gate_ref, rate_ref, res_ref, matrix_ref, pay_ref, halo_ref, next_ref):
-    where = Rows(g_ref.shape[0])
+def first_kernel(lags, g_ref, gate_ref, rate_ref, res_ref, moment_ref, pay_ref, halo_ref, next_ref, late_ref):
     next_ref[...] = jnp.concatenate([rate_ref[1], res_ref[1]], axis=0)
     taps = filter_nodes(rate_ref[0], res_ref[0], lags)
-    matrix = matrix_ref[where.moment, :]
+    matrix = moment_ref[...]
     for at, cut in tiles(g_ref.shape[1]):
         product = (gate_ref[0, :, cut].astype(F32) * g_ref[:, cut].astype(F32)).astype(BF)
         halo_ref[:, cut] = product[:16]
+        late_ref[:, cut] = gate_ref[1, :, cut]
         send_moments(product, matrix, taps, at, pay_ref)
 
 
-def scan_body(source, gaps, rows, rate, res, pay_ref, out_ref):
+def scan_body(source, gaps, rows, rate, res, pay_ref, out_ref, taps):
     low, top = low_lanes(), top_rows()
-    pairs = pay_ref.shape[0] // 16
+    width = HALF if taps is None else 2 * HALF
+    groups = pay_ref.shape[0] // 16
     rate, res = doubled(rate), doubled(res)
     enter = []
     for r in range(HALF):
@@ -164,8 +168,6 @@
         total = jnp.zeros((8, 128), F32)
         for m in range(MODES):
             total = total + leave[m] * state[m // 8][m % 8 : m % 8 + 1]
-        high = total.astype(BF).astype(F32)
-        total = jnp.where(top, high, total - high)
         sums = [None, None]
         for o in range(2):
             part = enter[0][o] * block[0:1]
@@ -174,25 +176,30 @@
             sums[o] = part + pltpu.roll(part, 64, 1)
         return total, tuple(step[o] * state[o] + sums[o] for o in range(2))
 
-    def pair(i, state):
-        place = pl.ds(pl.multiple_of((pairs - 1 - i) * 16, 16), 16)
+    def several(i, state):
+        place = pl.ds(pl.multiple_of((groups - 1 - i) * 16, 16), 16)
         blocks = pay_ref[place, :].astype(F32)
-        later, state = one(blocks[8:], state)
-        earlier, state = one(blocks[:8], state)
-        out_ref[place, :] = jnp.concatenate([earlier, later], axis=0).astype(BF)
+        outs = [None] * (16 // width)
+        for k in reversed(range(len(outs))):
+            outs[k], state = one(blocks[k * width : k * width + HALF], state)
+        if taps is None:
+            outs = [jnp.where(top, outs[k], outs[k + 1]) for k in range(0, len(outs), 2)]
+        else:
+            outs = [jnp.where(top, out, taps) for out in outs]
+        out_ref[place, :] = jnp.concatenate(outs, axis=0).astype(BF)
         return state
 
     zero = jnp.zeros((8, 128), F32)
-    lax.fori_loop(0, pairs, pair, (zero, zero), unroll=4)
-
-
-def scan_first_kernel(source, gaps, lags, rows, pay_ref, rate_ref, res_ref, next_ref, out_ref, taps_ref):
-    scan_body(source, gaps, rows, rate_ref[0], res_ref[0], pay_ref, out_ref)
-    taps_ref[...] = filter_nodes(next_ref[:MODES], next_ref[MODES:], lags)
+    lax.fori_loop(0, groups, several, (zero, zero), unroll=4 if width == 8 else 2)
+
+
+def scan_first_kernel(source, gaps, lags, rows, pay_ref, rate_ref, res_ref, next_ref, out_ref):
+    taps = filter_nodes(next_ref[:MODES], next_ref[MODES:], lags)
+    scan_body(source, gaps, rows, rate_ref[0], res_ref[0], pay_ref, out_ref, taps)
 
 
 def scan_last_kernel(source, gaps, rows, pay_ref, next_ref, out_ref):
-    scan_body(source, gaps, rows, next_ref[:MODES], next_ref[MODES:], pay_ref, out_ref)
+    scan_body(source, gaps, rows, next_ref[:MODES], next_ref[MODES:], pay_ref, out_ref, None)
 
 
 def inside_kernel(g_ref, gate_ref, halo_ref, pay_ref, matrix_ref, local_ref, rim_ref):
@@ -200,7 +207,8 @@
     where = Rows(rows)
     low = low_lanes()
     for at, cut in tiles(channels):
-        product = (gate_ref[0, :, cut].astype(F32) * g_ref[:, cut].astype(F32)).astype(BF)
+        gate = gate_ref[0, :, cut] if len(gate_ref.shape) == 3 else gate_ref[:, cut]
+        product = (gate.astype(F32) * g_ref[:, cut].astype(F32)).astype(BF)
         parts = []
         for t in range(at // 128, (at + TILE) // 128):
             both = pay_ref[t * 16 : t * 16 + 16, :].astype(F32)
@@ -221,14 +229,20 @@
 
 
 def updated_tile(at, cut, g_ref, local_ref, rim_ref, pay_ref, matrix, short):
-    rows = g_ref.shape[0]
-    low = low_lanes()
+    rows, channels = g_ref.shape
+    low, top = low_lanes(), top_rows()
     parts = []
     for t in range(at // 128, (at + TILE) // 128):
-        both = pay_ref[t * 16 : t * 16 + 16, :].astype(F32)
-        parts.append(jnp.concatenate(unpack(both[:8], both[8:], low), axis=0))
+        if pay_ref.shape[0] * 8 == channels:
+            both = pay_ref[t * 16 : t * 16 + 16, :].astype(F32)
+            first, second = unpack(both[:8], both[8:], low)
+        else:
+            both = pay_ref[t // 2 * 16 : t // 2 * 16 + 16, :].astype(F32)[t % 2 * 8 : t % 2 * 8 + 8]
+            first, second = unpack(both, pltpu.roll(both, HALF, 0), low)
+        parts.append(jnp.where(top, first, pltpu.roll(second, HALF, 0)))
     nodes = jnp.concatenate(parts, axis=1).astype(BF)
-    outside = jnp.dot(matrix, twice(nodes), preferred_element_type=F32)
+    nodes = jnp.concatenate([nodes, nodes], axis=0)
+    outside = jnp.dot(matrix, nodes, preferred_element_type=F32)
     carried = (local_ref[:, cut] + outside[:rows]).astype(BF).astype(F32)
     rim = (rim_ref[:, cut] + outside[rows:]).astype(BF).astype(F32)
     extended = jnp.concatenate([carried, rim], axis=0)
@@ -239,32 +253,29 @@
     return (g_ref[:, cut].astype(F32) + tail).astype(BF)
 
 
-def turn_kernel(g_ref, local_ref, rim_ref, nodes_ref, short_ref, gate_ref, matrix_ref, new_ref, pay_ref, halo_ref):
+def turn_kernel(
+    g_ref, local_ref, rim_ref, nodes_ref, short_ref, gate_ref, matrix_ref, gate_late, short_late,
+    new_ref, pay_ref, halo_ref,
+):
     where = Rows(g_ref.shape[0])
-    spread = matrix_ref[where.spread, :32]
+    spread = matrix_ref[where.spread, : 2 * NODES]
     moment = matrix_ref[where.moment, :]
-    none = jnp.zeros((8, 128), F32)
     for at, cut in tiles(g_ref.shape[1]):
         new = updated_tile(at, cut, g_ref, local_ref, rim_ref, nodes_ref, spread, short_ref[0, :, cut])
         new_ref[:, cut] = new
-        product = (gate_ref[0, :, cut].astype(F32) * new.astype(F32)).astype(BF)
+        product = (gate_ref[:, cut].astype(F32) * new.astype(F32)).astype(BF)
         halo_ref[:, cut] = product[:16]
-        send_moments(product, moment, none, at, pay_ref)
-
-
-def merge_kernel(pay_ref, taps_ref, g_ref, out_ref, same_ref):
-    top = top_rows()
-    taps = taps_ref[...]
-    for t in range(0, pay_ref.shape[0], 16):
-        both = pay_ref[t : t + 16, :].astype(F32)
-        block = jnp.concatenate([jnp.where(top, both[:8], taps), jnp.where(top, both[8:], taps)], axis=0)
-        out_ref[t : t + 16, :] = block.astype(BF)
+        send_moments(product, moment, None, at, pay_ref)
+
+
+def order_kernel(pay_ref, g_ref, out_ref, same_ref):
+    out_ref[...] = pay_ref[...]
 
 
 def last_kernel(g_ref, local_ref, rim_ref, nodes_ref, short_ref, matrix_ref, out_ref):
-    spread = matrix_ref[Rows(g_ref.shape[0]).spread, :32]
+    spread = matrix_ref[Rows(g_ref.shape[0]).spread, : 2 * NODES]
     for at, cut in tiles(g_ref.shape[1]):
-        out_ref[:, cut] = updated_tile(at, cut, g_ref, local_ref, rim_ref, nodes_ref, spread, short_ref[0, :, cut])
+        out_ref[:, cut] = updated_tile(at, cut, g_ref, local_ref, rim_ref, nodes_ref, spread, short_ref[:, cut])
 
 
 PARAMS = pltpu.CompilerParams(vmem_limit_bytes=VMEM_MIB * 1024 * 1024)
@@ -287,16 +298,21 @@
     )(*ins)
 
 
+def in_hbm(x):
+    return pltpu.with_memory_space_constraint(x, pltpu.HBM)
+
+
 def on_device(cotangent, gates, short_weight, decay_rates, residues):
-    g = cotangent[0]
-    gates = gates[0]
+    g = in_hbm(cotangent[0])
+    gates = in_hbm(gates[0])
     short_weight = short_weight[0]
-    rates = jnp.swapaxes(decay_rates[0], 1, 2)
-    weights = jnp.swapaxes(residues[0], 1, 2)
+    rates = in_hbm(jnp.swapaxes(decay_rates[0], 1, 2))
+    weights = in_hbm(jnp.swapaxes(residues[0], 1, 2))
     rows, channels = g.shape
     shards = lax.axis_size("seq")
     segments = lax.axis_size("segment")
     source, gaps, lags, matrices = constants(rows)
+    moment = in_hbm(jnp.asarray(matrices[Rows(rows).moment]))
     matrices = jnp.asarray(matrices)
 
     def shape(size, dtype):
@@ -306,59 +322,59 @@
         return lax.ppermute(x, "segment", [(i, (i + distance) % segments) for i in range(segments)])
 
     def across(x):
-        x = x.reshape(shards, 8, 128)
-        return lax.all_to_all(x, "seq", split_axis=0, concat_axis=0, tiled=True).reshape(shards * 8, 128)
-
-    pay_shape = shape((shards * 8, 128), BF)
+        blocks = x.reshape(shards, x.shape[0] // shards, 128)
+        return lax.all_to_all(blocks, "seq", split_axis=0, concat_axis=0, tiled=True).reshape(x.shape)
+
+    pay_shape = shape((shards * 2 * HALF, 128), BF)
+    short_pay_shape = shape((shards * HALF, 128), BF)
     halo_shape = shape((16, channels), BF)
     row_shape = shape((rows, channels), BF)
     local_shapes = [shape((rows, channels), F32), shape((8, channels), F32)]
     layer_gate = pl.BlockSpec((1, rows, channels), lambda i: (0, 0, 0))
     layer_short = pl.BlockSpec((1, SHORT, channels), lambda i: (0, 0, 0))
 
-    pay, halo, params = call(
-        first_kernel, "first", [g, gates, rates, weights, matrices],
-        [pay_shape, halo_shape, shape((2 * MODES, channels // shards), F32)],
-        fixed=(lags,), specs={1: layer_gate},
-    )
-    late_gates = gates[1:]
-    gates_early = around(late_gates, 1)
-    gates_late = around(late_gates, -1)
+    pay, halo, params, late_gates = call(
+        first_kernel, "first", [g, gates, rates, weights, moment],
+        [pay_shape, halo_shape, shape((2 * MODES, channels // shards), F32), row_shape],
+        fixed=(lags,),
+    )
+    gates_early = in_hbm(around(late_gates, 1))
+    gates_late = in_hbm(around(late_gates, -1))
     params_late = around(params, -1)
-    short_late = around(short_weight[1:], -1)
+    short_late = around(short_weight[1], -1)
     halo = lax.ppermute(halo, "seq", [(i, i - 1) for i in range(1, shards)])
     got = across(pay)
-    back, taps = call(
-        scan_first_kernel, "scan", [got, rates, weights, params_late],
-        [pay_shape, shape((8, 128), F32)], fixed=(source, gaps, lags, rows),
+    (back,) = call(
+        scan_first_kernel, "scan", [got, rates, weights, params_late], [pay_shape], fixed=(source, gaps, lags, rows)
     )
     nodes = across(back)
     local, rim = call(
         inside_kernel, "inside", [g, gates, halo, got, matrices], local_shapes, specs={1: layer_gate},
         flops=2 * NODES * rows * 2 * rows * channels,
     )
+    taps = nodes
+    anywhere = pl.BlockSpec(memory_space=pl.ANY)
     g, pay, halo = call(
-        turn_kernel, "turn", [g, local, rim, nodes, short_weight, gates_early, matrices],
-        [row_shape, pay_shape, halo_shape], specs={4: layer_short},
+        turn_kernel, "turn", [g, local, rim, nodes, short_weight, gates_early, matrices, gates_late, short_late],
+        [row_shape, short_pay_shape, halo_shape], specs={4: layer_short, 7: anywhere, 8: anywhere},
     )
     pay = around(pay, -2)
     moves = [
         (s * shards + k, (s - 2) % segments * shards + k - 1) for s in range(segments) for k in range(1, shards)
     ]
     halo = lax.ppermute(halo, ("segment", "seq"), moves)
-    anywhere = pl.BlockSpec(memory_space=pl.ANY)
     pay, g = call(
-        merge_kernel, "merge", [pay, taps, g], [pay_shape, row_shape],
-        specs={2: anywhere}, out_specs={1: anywhere}, aliases={2: 1},
-    )
-    g = around(g, -2)
+        order_kernel, "order", [pay, g], [short_pay_shape, row_shape],
+        specs={1: anywhere}, out_specs={1: anywhere}, aliases={1: 1},
+    )
+    g = in_hbm(around(g, -2))
     got = across(pay)
     (back,) = call(
-        scan_last_kernel, "scan", [got, params_late], [pay_shape], fixed=(source, gaps, rows)
+        scan_last_kernel, "scan", [got, params_late], [short_pay_shape], fixed=(source, gaps, rows)
     )
     nodes = across(back)
     local, rim = call(
-        inside_kernel, "inside", [g, gates_late, halo, got, matrices], local_shapes,
+        inside_kernel, "inside", [g, gates_late, halo, taps, matrices], local_shapes,
         flops=2 * NODES * rows * 2 * rows * channels,
     )
     (g,) = call(last_kernel, "last", [g, local, rim, nodes, short_late, matrices], [row_shape])

time: 147 us -> 129 us (0.88)
  local copies, waits for them, and re-layouts: 13.9 us -> 1.71 us
  waiting for transfers between devices: 52.6 us -> 44.1 us
  Pallas kernels: 21.3 us -> 28.6 us
  starting transfers between devices: 58.7 us -> 53.7 us
    ppermute x1, waiting for transfers between devices: 16.4 us -> 0.01 us  [on_device(): halo = lax.ppermute(halo, ('segment', 'seq'), moves)]
    all_to_all x4, waiting for transfers between devices: 26.5 us -> 42.2 us  [across(): lax.all_to_all(blocks, 'seq', split_axis=0, concat_axis=0, tiled=True)]
    unnamed x27 -> x9, local copies, waits for them, and re-layouts: 11.5 us -> 1.7 us
    all_to_all x4, starting transfers between devices: 43.9 us -> 35.7 us  [across(): lax.all_to_all(blocks, 'seq', split_axis=0, concat_axis=0, tiled=True)]
    pallas_call x8, Pallas kernels: 21.3 us -> 28.6 us  [call(): pl.pallas_call(lambda *refs: kernel(*fixed, *refs), grid=(1,), in_specs=[...]
    ppermute x1, waiting for transfers between devices: 4.33 us -> 0.01 us  [on_device(): halo = lax.ppermute(halo, 'seq', [(i, i - 1) for i in range(1, shards)])]
    ppermute x6, starting transfers between devices: 9.97 us -> 13.8 us  [around(): lax.ppermute(x, 'segment', [(i, (i + distance) % segments) for i in range...]
    ppermute x6, waiting for transfers between devices: 5.36 us -> 1.9 us  [around(): lax.ppermute(x, 'segment', [(i, (i + distance) % segments) for i in range...]
  transfers between devices with their start and end apart: 12 -> 12, of which waited for: 7 -> 5; matrix products, arithmetic and copies ran while one was open for 1% -> 0% of each run, Pallas kernels for 8% -> 10%
where the time goes in v1:
time: 129 us; the launch traced here: 128 us
  starting transfers between devices  53.7 us (42%)
  waiting for transfers between devices  44.1 us (34%)
  Pallas kernels  28.6 us (22%)
  local copies, waits for them, and re-layouts  1.71 us (1%)
    all_to_all x4, waiting for transfers between devices, across(): lax.all_to_all(blocks, 'seq', split_axis=0, concat_axis=0, tiled=True)  42.2 us
    all_to_all x4, starting transfers between devices, across(): lax.all_to_all(blocks, 'seq', split_axis=0, concat_axis=0, tiled=True)  35.7 us
    pallas_call x8, Pallas kernels, call(): pl.pallas_call(lambda *refs: kernel(*fixed, *refs), grid=(1,), in_specs=[...  28.6 us
    ppermute x6, starting transfers between devices, around(): lax.ppermute(x, 'segment', [(i, (i + distance) % segments) for i in range...  13.8 us
  transfers between devices with their start and end apart: 12, of which 5 were waited for; matrix products, arithmetic and copies ran while one was open for 0% of the time, Pallas kernels for 10%

profile of v1, /device:TPU:8, one launch (start us, length us, event | category | flops | bytes accessed | tf_op | source)
XLA Modules:
  0.0 128.3 jit_solution(16281179248893853504)
XLA Ops:
  0.0 0.0 copy-start.3
  0.0 0.0 copy-start
  0.0 3.4 %first.1 = (bf16[512,128]{1,0:T(8,128)(2,1)}, bf16[16,4096]{1,0:T(8,128)(2,1)S(1)}, f32[32,64]{1,0:T(8,128)S(1)}, bf16[128,4096]{1,0:T(8,128)(2,1)}) custom-call(bf16[128,4096]{1,0:T(8,128)(2,1)} %bitcast.28, bf16[2,128,4096]{2,1,0:T(8,128)(2,1)} %bitcast.31, f32[2,16,64]{2,1,0:T(8,128)} %bitcast.33, f32[2,16,64]{2,1,0:T(8,128)} %bitcast.35, ...), custom_call_target="tpu_custom_call" | custom-call | bytes 8388608 | tf_op jit(solution)/shard_map/first/pallas_call | solution.py:288
  3.5 18.7 %all-to-all-start = ((bf16[64,8,128]{2,1,0:T(8,128)(2,1)}), bf16[64,8,128]{2,1,0:T(8,128)(2,1)S(1)}, u32[]{:S(2)}, u32[]{:S(2)}) async-start(bf16[64,8,128]{2,1,0:T(8,128)(2,1)} %bitcast.6), calls=%async_computation | async-start | bytes 262144 | tf_op jit(solution)/shard_map/all_to_all | solution.py:326
  22.2 1.6 %collective-permute-start.1 = (f32[32,64]{1,0:T(8,128)S(1)}, f32[32,64]{1,0:T(8,128)S(1)}, u32[]{:S(2)}, u32[]{:S(2)}) collective-permute-start(f32[32,64]{1,0:T(8,128)S(1)} %get-tuple-element.22), channel_id=1, source_target_pairs={{0,448},{64,0},{128,64},{192,128},{256,192},{320,256},{384,320},{4... | collective-permute-start | bytes 24584 | tf_op jit(solution)/shard_map/ppermute | solution.py:322
  23.8 1.2 collective-permute-start.3
  25.1 0.0 collective-permute-start.2
  25.1 2.4 %collective-permute-start = (bf16[16,4096]{1,0:T(8,128)(2,1)S(1)}, bf16[16,4096]{1,0:T(8,128)(2,1)S(1)}, u32[]{:S(2)}, u32[]{:S(2)}) collective-permute-start(bf16[16,4096]{1,0:T(8,128)(2,1)S(1)} %get-tuple-element.18), channel_id=1, source_target_pairs={{1,0},{2,1},{3,2},{4,3},{5,4},{6,5},{7,6},{8,7},{9,8},{10,9},{11,1... | collective-permute-start | bytes 393224 | tf_op jit(solution)/shard_map/ppermute | solution.py:345
  27.4 0.0 copy-done.3
  27.4 0.1 copy.13
  27.6 0.0 collective-permute-done.1.refs_3_.refs_1_
  27.6 11.2 %all-to-all-done = bf16[64,8,128]{2,1,0:T(8,128)(2,1)S(1)} async-done(((bf16[64,8,128]{2,1,0:T(8,128)(2,1)}), bf16[64,8,128]{2,1,0:T(8,128)(2,1)S(1)}, u32[]{:S(2)}, u32[]{:S(2)}) %all-to-all-start) | async-done | bytes 131104 | tf_op jit(solution)/shard_map/all_to_all | solution.py:326
  38.8 2.6 %scan.2 = bf16[512,128]{1,0:T(8,128)(2,1)} custom-call(bf16[512,128]{1,0:T(8,128)(2,1)S(1)} %bitcast.24, f32[2,16,64]{2,1,0:T(8,128)} %bitcast.34, f32[2,16,64]{2,1,0:T(8,128)} %bitcast.36, f32[32,64]{1,0:T(8,128)S(1)} %collective-permute-done.1.refs_3_.refs_1_), custom_call_target="tpu_custom_call" | custom-call | bytes 8388608 | tf_op jit(solution)/shard_map/scan/pallas_call | solution.py:288
  41.4 5.6 %all-to-all-start.1 = ((bf16[64,8,128]{2,1,0:T(8,128)(2,1)}), bf16[64,8,128]{2,1,0:T(8,128)(2,1)S(1)}, u32[]{:S(2)}, u32[]{:S(2)}) async-start(bf16[64,8,128]{2,1,0:T(8,128)(2,1)} %bitcast.10), calls=%async_computation.1 | async-start | bytes 262144 | tf_op jit(solution)/shard_map/all_to_all | solution.py:326
  47.0 0.8 collective-permute-start.4
  47.8 0.0 collective-permute-done.refs_2_
  47.8 0.0 copy-start.1
  47.8 0.6 copy-done.1
  48.4 0.0 copy-done
  48.4 0.0 copy-start.2
  48.4 0.9 copy-done.2
  49.3 4.3 %inside.2 = (f32[128,4096]{1,0:T(8,128)S(1)}, f32[8,4096]{1,0:T(8,128)S(1)}) custom-call(bf16[128,4096]{1,0:T(8,128)(2,1)} %bitcast.29, bf16[2,128,4096]{2,1,0:T(8,128)(2,1)} %bitcast.32, bf16[16,4096]{1,0:T(8,128)(2,1)S(1)} %copy-done.2, bf16[512,128]{1,0:T(8,128)(2,1)S(1)} %bitcast.25, bf16[1240,256]{1,0:T(8,128)(2,1)S(1)} %copy-done), custom_call_target="tpu_custom_call" | custom-call | flops 2147483648 | bytes 8388608 | tf_op jit(solution)/shard_map/inside/pallas_call | solution.py:288
  53.7 0.0 collective-permute-done.4.refs_8_.refs_4_
  53.7 8.9 %all-to-all-done.1 = bf16[64,8,128]{2,1,0:T(8,128)(2,1)S(1)} async-done(((bf16[64,8,128]{2,1,0:T(8,128)(2,1)}), bf16[64,8,128]{2,1,0:T(8,128)(2,1)S(1)}, u32[]{:S(2)}, u32[]{:S(2)}) %all-to-all-start.1) | async-done | bytes 131104 | tf_op jit(solution)/shard_map/all_to_all | solution.py:326
  62.6 0.0 collective-permute-done.3.refs_7_.refs_1_
  62.6 0.0 collective-permute-done.2.refs_5_
  62.6 6.5 %turn.1 = (bf16[128,4096]{1,0:T(8,128)(2,1)}, bf16[256,128]{1,0:T(8,128)(2,1)S(1)}, bf16[16,4096]{1,0:T(8,128)(2,1)S(1)}) custom-call(bf16[128,4096]{1,0:T(8,128)(2,1)} %bitcast.30, f32[128,4096]{1,0:T(8,128)S(1)} %get-tuple-element.20.refs_1_, f32[8,4096]{1,0:T(8,128)S(1)} %get-tuple-element.21.refs_2_, bf16[512,128]{1,0:T(8,128)(2,1)S(1)} %bitcast.22, ...), custom_call_target="tpu_custom_call" | custom-call | bytes 8388608 | tf_op jit(solution)/shard_map/turn/pallas_call | solution.py:288
  69.1 4.7 %collective-permute-start.5 = (bf16[256,128]{1,0:T(8,128)(2,1)S(1)}, bf16[256,128]{1,0:T(8,128)(2,1)S(1)}, u32[]{:S(2)}, u32[]{:S(2)}) collective-permute-start(bf16[256,128]{1,0:T(8,128)(2,1)S(1)} %get-tuple-element.24), channel_id=1, source_target_pairs={{0,384},{64,448},{128,0},{192,64},{256,128},{320,192},{384,256},{4... | collective-permute-start | bytes 196616 | tf_op jit(solution)/shard_map/ppermute | solution.py:322
  73.8 1.9 %collective-permute-done.5.refs_0_ = bf16[256,128]{1,0:T(8,128)(2,1)S(1)} collective-permute-done((bf16[256,128]{1,0:T(8,128)(2,1)S(1)}, bf16[256,128]{1,0:T(8,128)(2,1)S(1)}, u32[]{:S(2)}, u32[]{:S(2)}) %collective-permute-start.5) | collective-permute-done | bytes 65568 | tf_op jit(solution)/shard_map/ppermute | solution.py:322
  75.7 0.6 order.1
  76.3 5.5 %collective-permute-start.6 = (bf16[128,4096]{1,0:T(8,128)(2,1)}, bf16[128,4096]{1,0:T(8,128)(2,1)}, u32[]{:S(2)}, u32[]{:S(2)}) collective-permute-start(bf16[128,4096]{1,0:T(8,128)(2,1)} %get-tuple-element.26), channel_id=1, source_target_pairs={{0,384},{64,448},{128,0},{192,64},{256,128},{320,192},{384,256},{4... | collective-permute-start | bytes 3145736 | tf_op jit(solution)/shard_map/ppermute | solution.py:322
  81.8 5.8 %all-to-all-start.2 = ((bf16[64,4,128]{2,1,0:T(4,128)(2,1)}), bf16[64,4,128]{2,1,0:T(4,128)(2,1)S(1)}, u32[]{:S(2)}, u32[]{:S(2)}) async-start(bf16[64,4,128]{2,1,0:T(4,128)(2,1)} %bitcast.14), calls=%async_computation.2 | async-start | bytes 131072 | tf_op jit(solution)/shard_map/all_to_all | solution.py:326
  87.6 1.9 %collective-permute-start.7 = (bf16[16,4096]{1,0:T(8,128)(2,1)S(1)}, bf16[16,4096]{1,0:T(8,128)(2,1)S(1)}, u32[]{:S(2)}, u32[]{:S(2)}) collective-permute-start(bf16[16,4096]{1,0:T(8,128)(2,1)S(1)} %get-tuple-element.27), channel_id=1, source_target_pairs={{1,384},{2,385},{3,386},{4,387},{5,388},{6,389},{7,390},{8,391},{9... | collective-permute-start | bytes 393224 | tf_op jit(solution)/shard_map/ppermute | solution.py:365
  89.5 12.2 %all-to-all-done.2 = bf16[64,4,128]{2,1,0:T(4,128)(2,1)S(1)} async-done(((bf16[64,4,128]{2,1,0:T(4,128)(2,1)}), bf16[64,4,128]{2,1,0:T(4,128)(2,1)S(1)}, u32[]{:S(2)}, u32[]{:S(2)}) %all-to-all-start.2) | async-done | bytes 65568 | tf_op jit(solution)/shard_map/all_to_all | solution.py:326
  101.8 1.8 %scan.3 = bf16[256,128]{1,0:T(8,128)(2,1)} custom-call(bf16[256,128]{1,0:T(8,128)(2,1)S(1)} %bitcast.27, f32[32,64]{1,0:T(8,128)S(1)} %collective-permute-done.1.refs_3_.refs_1_), custom_call_target="tpu_custom_call" | custom-call | bytes 8388608 | tf_op jit(solution)/shard_map/scan/pallas_call | solution.py:288
  103.6 5.5 %all-to-all-start.3 = ((bf16[64,4,128]{2,1,0:T(4,128)(2,1)}), bf16[64,4,128]{2,1,0:T(4,128)(2,1)S(1)}, u32[]{:S(2)}, u32[]{:S(2)}) async-start(bf16[64,4,128]{2,1,0:T(4,128)(2,1)} %bitcast.16), calls=%async_computation.3 | async-start | bytes 131072 | tf_op jit(solution)/shard_map/all_to_all | solution.py:326
  109.1 0.0 collective-permute-done.7.refs_2_
  109.1 0.0 collective-permute-done.6.refs_0_
  109.1 4.4 %inside.3 = (f32[128,4096]{1,0:T(8,128)S(1)}, f32[8,4096]{1,0:T(8,128)S(1)}) custom-call(bf16[128,4096]{1,0:T(8,128)(2,1)} %collective-permute-done.6.refs_0_, bf16[128,4096]{1,0:T(8,128)(2,1)} %collective-permute-done.3.refs_7_.refs_1_, bf16[16,4096]{1,0:T(8,128)(2,1)S(1)} %collective-permute-done.7.refs_2_, bf16[512,128]{1,0:T(8,128)(2,1)S(1)} %bitcast.23, ...), custom_call_target="tpu_custom_call" | custom-call | flops 2147483648 | bytes 8388608 | tf_op jit(solution)/shard_map/inside/pallas_call | solution.py:288
  113.5 9.9 %all-to-all-done.3 = bf16[64,4,128]{2,1,0:T(4,128)(2,1)S(1)} async-done(((bf16[64,4,128]{2,1,0:T(4,128)(2,1)}), bf16[64,4,128]{2,1,0:T(4,128)(2,1)S(1)}, u32[]{:S(2)}, u32[]{:S(2)}) %all-to-all-start.3) | async-done | bytes 65568 | tf_op jit(solution)/shard_map/all_to_all | solution.py:326
  123.4 4.9 %last.1 = bf16[128,4096]{1,0:T(8,128)(2,1)} custom-call(bf16[128,4096]{1,0:T(8,128)(2,1)} %collective-permute-done.6.refs_0_, f32[128,4096]{1,0:T(8,128)S(1)} %get-tuple-element.28.refs_1_, f32[8,4096]{1,0:T(8,128)S(1)} %get-tuple-element.29.refs_2_, bf16[256,128]{1,0:T(8,128)(2,1)S(1)} %bitcast.26, f32[7,4096]{1,0:T(8,128)S(1)} %collective-permute-done.4.refs_8_.refs_4_, ...), custom_call_target="tpu_custom_call" | custom-call | bytes 8388608 | tf_op jit(solution)/shard_map/last/pallas_call | solution.py:288
  (1 shorter events, 0.0 us)
Async XLA Ops:
  0.0 27.4 %copy-start.3 = (f32[1,2,7,4096]{3,1,2,0:T(2,128)S(1)}, f32[1,2,7,4096]{3,1,2,0:T(2,128)}, u32[]{:S(2)}) copy-start(f32[1,2,7,4096]{3,1,2,0:T(2,128)} %param.9) | copy-start | bytes 688132
  0.0 48.4 %copy-start = (bf16[1240,256]{1,0:T(8,128)(2,1)S(1)}, bf16[1240,256]{1,0:T(8,128)(2,1)}, u32[]{:S(2)}) copy-start(bf16[1240,256]{1,0:T(8,128)(2,1)} %constant.5.clone.refs_4_.refs_6_.refs_5_) | copy-start | bytes 1904644
  3.5 35.3 %all-to-all-start = ((bf16[64,8,128]{2,1,0:T(8,128)(2,1)}), bf16[64,8,128]{2,1,0:T(8,128)(2,1)S(1)}, u32[]{:S(2)}, u32[]{:S(2)}) async-start(bf16[64,8,128]{2,1,0:T(8,128)(2,1)} %bitcast.6), calls=%async_computation | async-start | bytes 262144 | tf_op jit(solution)/shard_map/all_to_all | solution.py:326
  22.2 5.4 %collective-permute-start.1 = (f32[32,64]{1,0:T(8,128)S(1)}, f32[32,64]{1,0:T(8,128)S(1)}, u32[]{:S(2)}, u32[]{:S(2)}) collective-permute-start(f32[32,64]{1,0:T(8,128)S(1)} %get-tuple-element.22), channel_id=1, source_target_pairs={{0,448},{64,0},{128,64},{192,128},{256,192},{320,256},{384,320},{4... | collective-permute-start | bytes 24584 | tf_op jit(solution)/shard_map/ppermute | solution.py:322
  23.8 38.7 %collective-permute-start.3 = (bf16[128,4096]{1,0:T(8,128)(2,1)}, bf16[128,4096]{1,0:T(8,128)(2,1)}, u32[]{:S(2)}, u32[]{:S(2)}) collective-permute-start(bf16[128,4096]{1,0:T(8,128)(2,1)} %get-tuple-element.23), channel_id=1, source_target_pairs={{0,448},{64,0},{128,64},{192,128},{256,192},{320,256},{384,320},{4... | collective-permute-start | bytes 3145736 | tf_op jit(solution)/shard_map/ppermute | solution.py:322
  25.1 37.5 %collective-permute-start.2 = (bf16[128,4096]{1,0:T(8,128)(2,1)}, bf16[128,4096]{1,0:T(8,128)(2,1)}, u32[]{:S(2)}, u32[]{:S(2)}) collective-permute-start(bf16[128,4096]{1,0:T(8,128)(2,1)} %get-tuple-element.23), channel_id=1, source_target_pairs={{0,64},{64,128},{128,192},{192,256},{256,320},{320,384},{384,448},... | collective-permute-start | bytes 3145736 | tf_op jit(solution)/shard_map/ppermute | solution.py:322
  25.1 22.7 %collective-permute-start = (bf16[16,4096]{1,0:T(8,128)(2,1)S(1)}, bf16[16,4096]{1,0:T(8,128)(2,1)S(1)}, u32[]{:S(2)}, u32[]{:S(2)}) collective-permute-start(bf16[16,4096]{1,0:T(8,128)(2,1)S(1)} %get-tuple-element.18), channel_id=1, source_target_pairs={{1,0},{2,1},{3,2},{4,3},{5,4},{6,5},{7,6},{8,7},{9,8},{10,9},{11,1... | collective-permute-start | bytes 393224 | tf_op jit(solution)/shard_map/ppermute | solution.py:345
  41.4 21.2 %all-to-all-start.1 = ((bf16[64,8,128]{2,1,0:T(8,128)(2,1)}), bf16[64,8,128]{2,1,0:T(8,128)(2,1)S(1)}, u32[]{:S(2)}, u32[]{:S(2)}) async-start(bf16[64,8,128]{2,1,0:T(8,128)(2,1)} %bitcast.10), calls=%async_computation.1 | async-start | bytes 262144 | tf_op jit(solution)/shard_map/all_to_all | solution.py:326
  47.0 6.7 %collective-permute-start.4 = (f32[7,4096]{1,0:T(8,128)S(1)}, f32[7,4096]{1,0:T(8,128)S(1)}, u32[]{:S(2)}, u32[]{:S(2)}) collective-permute-start(f32[7,4096]{1,0:T(8,128)S(1)} %slice_bitcast_fusion), channel_id=1, source_target_pairs={{0,448},{64,0},{128,64},{192,128},{256,192},{320,256},{384,320},{4... | collective-permute-start | bytes 344072 | tf_op jit(solution)/shard_map/ppermute | solution.py:322
  47.8 0.6 copy-start.1
  48.4 0.9 copy-start.2
  69.1 6.5 %collective-permute-start.5 = (bf16[256,128]{1,0:T(8,128)(2,1)S(1)}, bf16[256,128]{1,0:T(8,128)(2,1)S(1)}, u32[]{:S(2)}, u32[]{:S(2)}) collective-permute-start(bf16[256,128]{1,0:T(8,128)(2,1)S(1)} %get-tuple-element.24), channel_id=1, source_target_pairs={{0,384},{64,448},{128,0},{192,64},{256,128},{320,192},{384,256},{4... | collective-permute-start | bytes 196616 | tf_op jit(solution)/shard_map/ppermute | solution.py:322
  76.3 32.8 %collective-permute-start.6 = (bf16[128,4096]{1,0:T(8,128)(2,1)}, bf16[128,4096]{1,0:T(8,128)(2,1)}, u32[]{:S(2)}, u32[]{:S(2)}) collective-permute-start(bf16[128,4096]{1,0:T(8,128)(2,1)} %get-tuple-element.26), channel_id=1, source_target_pairs={{0,384},{64,448},{128,0},{192,64},{256,128},{320,192},{384,256},{4... | collective-permute-start | bytes 3145736 | tf_op jit(solution)/shard_map/ppermute | solution.py:322
  81.8 20.0 %all-to-all-start.2 = ((bf16[64,4,128]{2,1,0:T(4,128)(2,1)}), bf16[64,4,128]{2,1,0:T(4,128)(2,1)S(1)}, u32[]{:S(2)}, u32[]{:S(2)}) async-start(bf16[64,4,128]{2,1,0:T(4,128)(2,1)} %bitcast.14), calls=%async_computation.2 | async-start | bytes 131072 | tf_op jit(solution)/shard_map/all_to_all | solution.py:326
  87.6 21.5 %collective-permute-start.7 = (bf16[16,4096]{1,0:T(8,128)(2,1)S(1)}, bf16[16,4096]{1,0:T(8,128)(2,1)S(1)}, u32[]{:S(2)}, u32[]{:S(2)}) collective-permute-start(bf16[16,4096]{1,0:T(8,128)(2,1)S(1)} %get-tuple-element.27), channel_id=1, source_target_pairs={{1,384},{2,385},{3,386},{4,387},{5,388},{6,389},{7,390},{8,391},{9... | collective-permute-start | bytes 393224 | tf_op jit(solution)/shard_map/ppermute | solution.py:365
  103.6 19.8 %all-to-all-start.3 = ((bf16[64,4,128]{2,1,0:T(4,128)(2,1)}), bf16[64,4,128]{2,1,0:T(4,128)(2,1)S(1)}, u32[]{:S(2)}, u32[]{:S(2)}) async-start(bf16[64,4,128]{2,1,0:T(4,128)(2,1)} %bitcast.16), calls=%async_computation.3 | async-start | bytes 131072 | tf_op jit(solution)/shard_map/all_to_all | solution.py:326

commit v2 on v1

--- a/solution.py
+++ b/solution.py
@@ -228,8 +228,24 @@
         rim_ref[:, cut] = rim
 
 
-def updated_tile(at, cut, g_ref, local_ref, rim_ref, pay_ref, matrix, short):
-    rows, channels = g_ref.shape
+class Fetch:
+    def __init__(self, far, near, sems):
+        self.near = near
+        self.copies = [
+            pltpu.make_async_copy(far.at[:, cut], near.at[:, cut], sems.at[k])
+            for k, (_, cut) in enumerate(tiles(near.shape[1]))
+        ]
+
+    def start(self, at):
+        self.copies[at // TILE].start()
+
+    def tile(self, at):
+        self.copies[at // TILE].wait()
+        return self.near[:, at : at + TILE].astype(F32)
+
+
+def updated_tile(at, cut, g, local_ref, rim_ref, pay_ref, matrix, short):
+    rows, channels = g.near.shape
     low, top = low_lanes(), top_rows()
     parts = []
     for t in range(at // 128, (at + TILE) // 128):
@@ -250,48 +266,61 @@
     for j in range(SHORT):
         term = short[j : j + 1] * extended[j : j + rows]
         tail = term if tail is None else tail + term
-    return (g_ref[:, cut].astype(F32) + tail).astype(BF)
+    return (g.tile(at) + tail).astype(BF)
 
 
 def turn_kernel(
-    g_ref, local_ref, rim_ref, nodes_ref, short_ref, gate_ref, matrix_ref, gate_late, short_late,
-    new_ref, pay_ref, halo_ref,
+    g_far, local_ref, rim_ref, nodes_ref, short_ref, gate_far, matrix_ref, gate_late, short_late,
+    new_far, pay_ref, halo_ref, g_near, gate_near, new_near, g_sem, gate_sem, new_sem,
 ):
-    where = Rows(g_ref.shape[0])
+    where = Rows(g_near.shape[0])
+    g, gate = Fetch(g_far, g_near, g_sem), Fetch(gate_far, gate_near, gate_sem)
+    out = Fetch(new_near, new_far, new_sem)
+    for at, _ in tiles(g_near.shape[1]):
+        g.start(at)
+        gate.start(at)
     spread = matrix_ref[where.spread, : 2 * NODES]
     moment = matrix_ref[where.moment, :]
-    for at, cut in tiles(g_ref.shape[1]):
-        new = updated_tile(at, cut, g_ref, local_ref, rim_ref, nodes_ref, spread, short_ref[0, :, cut])
-        new_ref[:, cut] = new
-        product = (gate_ref[:, cut].astype(F32) * new.astype(F32)).astype(BF)
+    for at, cut in tiles(g_near.shape[1]):
+        new = updated_tile(at, cut, g, local_ref, rim_ref, nodes_ref, spread, short_ref[0, :, cut])
+        new_near[:, cut] = new
+        out.start(at)
+        product = (gate.tile(at) * new.astype(F32)).astype(BF)
         halo_ref[:, cut] = product[:16]
         send_moments(product, moment, None, at, pay_ref)
-
-
-def order_kernel(pay_ref, g_ref, out_ref, same_ref):
-    out_ref[...] = pay_ref[...]
-
-
-def last_kernel(g_ref, local_ref, rim_ref, nodes_ref, short_ref, matrix_ref, out_ref):
-    spread = matrix_ref[Rows(g_ref.shape[0]).spread, : 2 * NODES]
-    for at, cut in tiles(g_ref.shape[1]):
-        out_ref[:, cut] = updated_tile(at, cut, g_ref, local_ref, rim_ref, nodes_ref, spread, short_ref[:, cut])
+    for copy in out.copies:
+        copy.wait()
+
+
+def last_kernel(
+    g_far, local_ref, rim_ref, nodes_ref, short_ref, matrix_ref, out_far, g_near, out_near, g_sem, out_sem
+):
+    spread = matrix_ref[Rows(g_near.shape[0]).spread, : 2 * NODES]
+    g, out = Fetch(g_far, g_near, g_sem), Fetch(out_near, out_far, out_sem)
+    for at, _ in tiles(g_near.shape[1]):
+        g.start(at)
+    for at, cut in tiles(g_near.shape[1]):
+        out_near[:, cut] = updated_tile(at, cut, g, local_ref, rim_ref, nodes_ref, spread, short_ref[:, cut])
+        out.start(at)
+    for copy in out.copies:
+        copy.wait()
 
 
 PARAMS = pltpu.CompilerParams(vmem_limit_bytes=VMEM_MIB * 1024 * 1024)
 
 
-def call(kernel, name, ins, outs, fixed=(), layer=0, specs=None, out_specs=None, aliases=None, flops=0):
+def call(kernel, name, ins, outs, fixed=(), specs=None, out_specs=None, flops=0, scratch=None):
     def whole(array):
+        if scratch:
+            return pl.BlockSpec(memory_space=pltpu.VMEM)
         return pl.BlockSpec(array.shape, lambda i: (0,) * len(array.shape))
 
     return pl.pallas_call(
         lambda *refs: kernel(*fixed, *refs),
-        grid=(1,),
+        **({"scratch_shapes": scratch} if scratch else {"grid": (1,)}),
         in_specs=[(specs or {}).get(k) or whole(x) for k, x in enumerate(ins)],
         out_specs=[(out_specs or {}).get(k) or whole(x) for k, x in enumerate(outs)],
         out_shape=list(outs),
-        input_output_aliases=aliases or {},
         compiler_params=PARAMS,
         cost_estimate=pl.CostEstimate(flops=flops, bytes_accessed=8 * 2**20, transcendentals=0),
         name=name,
@@ -331,7 +360,6 @@
     row_shape = shape((rows, channels), BF)
     local_shapes = [shape((rows, channels), F32), shape((8, channels), F32)]
     layer_gate = pl.BlockSpec((1, rows, channels), lambda i: (0, 0, 0))
-    layer_short = pl.BlockSpec((1, SHORT, channels), lambda i: (0, 0, 0))
 
     pay, halo, params, late_gates = call(
         first_kernel, "first", [g, gates, rates, weights, moment],
@@ -341,6 +369,7 @@
     gates_early = in_hbm(around(late_gates, 1))
     gates_late = in_hbm(around(late_gates, -1))
     params_late = around(params, -1)
+    params_early = around(params, 1)
     short_late = around(short_weight[1], -1)
     halo = lax.ppermute(halo, "seq", [(i, i - 1) for i in range(1, shards)])
     got = across(pay)
@@ -354,30 +383,32 @@
     )
     taps = nodes
     anywhere = pl.BlockSpec(memory_space=pl.ANY)
+    near = [pltpu.VMEM((rows, channels), BF)]
+    sems = [pltpu.SemaphoreType.DMA((channels // TILE,))]
     g, pay, halo = call(
         turn_kernel, "turn", [g, local, rim, nodes, short_weight, gates_early, matrices, gates_late, short_late],
-        [row_shape, short_pay_shape, halo_shape], specs={4: layer_short, 7: anywhere, 8: anywhere},
-    )
-    pay = around(pay, -2)
+        [row_shape, short_pay_shape, halo_shape],
+        specs={0: anywhere, 5: anywhere, 7: anywhere, 8: anywhere}, out_specs={0: anywhere},
+        scratch=near * 3 + sems * 3,
+    )
     moves = [
         (s * shards + k, (s - 2) % segments * shards + k - 1) for s in range(segments) for k in range(1, shards)
     ]
     halo = lax.ppermute(halo, ("segment", "seq"), moves)
-    pay, g = call(
-        order_kernel, "order", [pay, g], [short_pay_shape, row_shape],
-        specs={1: anywhere}, out_specs={1: anywhere}, aliases={1: 1},
-    )
     g = in_hbm(around(g, -2))
     got = across(pay)
     (back,) = call(
-        scan_last_kernel, "scan", [got, params_late], [short_pay_shape], fixed=(source, gaps, rows)
-    )
-    nodes = across(back)
+        scan_last_kernel, "scan", [got, params_early], [short_pay_shape], fixed=(source, gaps, rows)
+    )
+    nodes = around(across(back), -2)
     local, rim = call(
         inside_kernel, "inside", [g, gates_late, halo, taps, matrices], local_shapes,
         flops=2 * NODES * rows * 2 * rows * channels,
     )
-    (g,) = call(last_kernel, "last", [g, local, rim, nodes, short_late, matrices], [row_shape])
+    (g,) = call(
+        last_kernel, "last", [g, local, rim, nodes, short_late, matrices], [row_shape],
+        specs={0: anywhere}, out_specs={0: anywhere}, scratch=near * 2 + sems * 2,
+    )
     return g[None]
 
 

time: 129 us -> 130 us (level)
  the two profiles are of different devices: /device:TPU:8 before, /device:TPU:2 now
where the time goes in v2:
time: 130 us; the launch traced here: 129 us
  waiting for transfers between devices  55.5 us (43%)
  starting transfers between devices  43.1 us (33%)
  Pallas kernels  27.8 us (21%)
  local copies, waits for them, and re-layouts  2.66 us (2%)
    all_to_all x4, waiting for transfers between devices, across(): lax.all_to_all(blocks, 'seq', split_axis=0, concat_axis=0, tiled=True)  52.4 us
    all_to_all x4, starting transfers between devices, across(): lax.all_to_all(blocks, 'seq', split_axis=0, concat_axis=0, tiled=True)  32.9 us
    pallas_call x7, Pallas kernels, call(): pl.pallas_call(lambda *refs: kernel(*fixed, *refs), **{'scratch_shapes':...  27.8 us
    ppermute x7, starting transfers between devices, around(): lax.ppermute(x, 'segment', [(i, (i + distance) % segments) for i in range...  7.58 us
    ppermute x7, waiting for transfers between devices, around(): lax.ppermute(x, 'segment', [(i, (i + distance) % segments) for i in range...  3.17 us
    unnamed x11, local copies, waits for them, and re-layouts  2.65 us
  transfers between devices with their start and end apart: 13, of which 5 were waited for; matrix products, arithmetic and copies ran while one was open for 0% of the time, Pallas kernels for 10%

profile of v2, /device:TPU:2, one launch (start us, length us, event | category | flops | bytes accessed | tf_op | source)
XLA Modules:
  0.0 129.4 jit_solution(17005318445392930110)
XLA Ops:
  0.0 0.0 copy-start.4
  0.0 0.0 copy-start
  0.0 3.4 %first.1 = (bf16[512,128]{1,0:T(8,128)(2,1)}, bf16[16,4096]{1,0:T(8,128)(2,1)S(1)}, f32[32,64]{1,0:T(8,128)S(1)}, bf16[128,4096]{1,0:T(8,128)(2,1)}) custom-call(bf16[128,4096]{1,0:T(8,128)(2,1)} %bitcast.27, bf16[2,128,4096]{2,1,0:T(8,128)(2,1)} %bitcast.30, f32[2,16,64]{2,1,0:T(8,128)} %bitcast.32, f32[2,16,64]{2,1,0:T(8,128)} %bitcast.34, ...), custom_call_target="tpu_custom_call" | custom-call | bytes 8388608 | tf_op jit(solution)/shard_map/first/pallas_call | solution.py:318
  3.4 18.7 %all-to-all-start = ((bf16[64,8,128]{2,1,0:T(8,128)(2,1)}), bf16[64,8,128]{2,1,0:T(8,128)(2,1)S(1)}, u32[]{:S(2)}, u32[]{:S(2)}) async-start(bf16[64,8,128]{2,1,0:T(8,128)(2,1)} %bitcast.6), calls=%async_computation | async-start | bytes 262144 | tf_op jit(solution)/shard_map/all_to_all | solution.py:355
  22.2 0.0 collective-permute-start.1
  22.2 0.6 collective-permute-start.3
  22.8 0.0 collective-permute-start.2
  22.9 1.3 collective-permute-start
  24.1 0.0 copy-done.4
  24.1 0.1 copy.12
  24.3 0.0 collective-permute-done.1.refs_3_
  24.3 15.6 %all-to-all-done = bf16[64,8,128]{2,1,0:T(8,128)(2,1)S(1)} async-done(((bf16[64,8,128]{2,1,0:T(8,128)(2,1)}), bf16[64,8,128]{2,1,0:T(8,128)(2,1)S(1)}, u32[]{:S(2)}, u32[]{:S(2)}) %all-to-all-start) | async-done | bytes 131104 | tf_op jit(solution)/shard_map/all_to_all | solution.py:355
  39.9 2.6 %scan.2 = bf16[512,128]{1,0:T(8,128)(2,1)} custom-call(bf16[512,128]{1,0:T(8,128)(2,1)S(1)} %bitcast.24, f32[2,16,64]{2,1,0:T(8,128)} %bitcast.33, f32[2,16,64]{2,1,0:T(8,128)} %bitcast.35, f32[32,64]{1,0:T(8,128)S(1)} %collective-permute-done.1.refs_3_), custom_call_target="tpu_custom_call" | custom-call | bytes 8388608 | tf_op jit(solution)/shard_map/scan/pallas_call | solution.py:318
  42.5 4.6 %all-to-all-start.1 = ((bf16[64,8,128]{2,1,0:T(8,128)(2,1)}), bf16[64,8,128]{2,1,0:T(8,128)(2,1)S(1)}, u32[]{:S(2)}, u32[]{:S(2)}) async-start(bf16[64,8,128]{2,1,0:T(8,128)(2,1)} %bitcast.10), calls=%async_computation.1 | async-start | bytes 262144 | tf_op jit(solution)/shard_map/all_to_all | solution.py:355
  47.1 0.0 collective-permute-start.4
  47.1 0.0 collective-permute-done.refs_2_
  47.1 0.0 copy-start.1
  47.1 0.6 copy-done.1
  47.8 0.0 copy-done
  47.8 0.0 copy-start.2
  47.8 0.9 copy-done.2
  48.7 4.3 %inside.2 = (f32[128,4096]{1,0:T(8,128)S(1)}, f32[8,4096]{1,0:T(8,128)S(1)}) custom-call(bf16[128,4096]{1,0:T(8,128)(2,1)} %bitcast.28, bf16[2,128,4096]{2,1,0:T(8,128)(2,1)} %bitcast.31, bf16[16,4096]{1,0:T(8,128)(2,1)S(1)} %copy-done.2, bf16[512,128]{1,0:T(8,128)(2,1)S(1)} %bitcast.25, bf16[1240,256]{1,0:T(8,128)(2,1)S(1)} %copy-done), custom_call_target="tpu_custom_call" | custom-call | flops 2147483648 | bytes 8388608 | tf_op jit(solution)/shard_map/inside/pallas_call | solution.py:318
  53.0 0.0 collective-permute-done.4.refs_8_.refs_4_
  53.0 10.8 %all-to-all-done.1 = bf16[64,8,128]{2,1,0:T(8,128)(2,1)S(1)} async-done(((bf16[64,8,128]{2,1,0:T(8,128)(2,1)}), bf16[64,8,128]{2,1,0:T(8,128)(2,1)S(1)}, u32[]{:S(2)}, u32[]{:S(2)}) %all-to-all-start.1) | async-done | bytes 131104 | tf_op jit(solution)/shard_map/all_to_all | solution.py:355
  63.8 0.0 collective-permute-done.3.refs_7_.refs_1_
  63.8 0.0 collective-permute-done.2.refs_5_
  63.8 6.0 %turn.1 = (bf16[128,4096]{1,0:T(8,128)(2,1)}, bf16[256,128]{1,0:T(8,128)(2,1)}, bf16[16,4096]{1,0:T(8,128)(2,1)S(1)}) custom-call(bf16[128,4096]{1,0:T(8,128)(2,1)} %bitcast.29, f32[128,4096]{1,0:T(8,128)S(1)} %get-tuple-element.18.refs_1_, f32[8,4096]{1,0:T(8,128)S(1)} %get-tuple-element.19.refs_2_, bf16[512,128]{1,0:T(8,128)(2,1)S(1)} %bitcast.22, ...), custom_call_target="tpu_custom_call" | custom-call | bytes 8388608 | tf_op jit(solution)/shard_map/turn/pallas_call | solution.py:318
  69.9 2.4 %collective-permute-start.5 = (bf16[128,4096]{1,0:T(8,128)(2,1)}, bf16[128,4096]{1,0:T(8,128)(2,1)S(1)}, u32[]{:S(2)}, u32[]{:S(2)}) collective-permute-start(bf16[128,4096]{1,0:T(8,128)(2,1)} %get-tuple-element.22), channel_id=1, source_target_pairs={{0,384},{64,448},{128,0},{192,64},{256,128},{320,192},{384,256},{4... | collective-permute-start | bytes 3145736 | tf_op jit(solution)/shard_map/ppermute | solution.py:351
  72.3 5.0 %all-to-all-start.2 = ((bf16[64,4,128]{2,1,0:T(4,128)(2,1)}), bf16[64,4,128]{2,1,0:T(4,128)(2,1)S(1)}, u32[]{:S(2)}, u32[]{:S(2)}) async-start(bf16[64,4,128]{2,1,0:T(4,128)(2,1)} %bitcast.14), calls=%async_computation.2 | async-start | bytes 131072 | tf_op jit(solution)/shard_map/all_to_all | solution.py:355
  77.3 0.0 collective-permute-start.7
  77.3 3.2 %collective-permute-done.7.refs_1_ = f32[32,64]{1,0:T(8,128)S(1)} collective-permute-done((f32[32,64]{1,0:T(8,128)S(1)}, f32[32,64]{1,0:T(8,128)S(1)}, u32[]{:S(2)}, u32[]{:S(2)}) %collective-permute-start.7) | collective-permute-done | bytes 8224 | tf_op jit(solution)/shard_map/ppermute | solution.py:351
  80.5 12.1 %all-to-all-done.2 = bf16[64,4,128]{2,1,0:T(4,128)(2,1)S(1)} async-done(((bf16[64,4,128]{2,1,0:T(4,128)(2,1)}), bf16[64,4,128]{2,1,0:T(4,128)(2,1)S(1)}, u32[]{:S(2)}, u32[]{:S(2)}) %all-to-all-start.2) | async-done | bytes 65568 | tf_op jit(solution)/shard_map/all_to_all | solution.py:355
  92.6 1.8 %scan.3 = bf16[256,128]{1,0:T(8,128)(2,1)} custom-call(bf16[256,128]{1,0:T(8,128)(2,1)S(1)} %bitcast.26, f32[32,64]{1,0:T(8,128)S(1)} %collective-permute-done.7.refs_1_), custom_call_target="tpu_custom_call" | custom-call | bytes 8388608 | tf_op jit(solution)/shard_map/scan/pallas_call | solution.py:318
  94.4 4.6 %all-to-all-start.3 = ((bf16[64,4,128]{2,1,0:T(4,128)(2,1)}), bf16[64,4,128]{2,1,0:T(4,128)(2,1)S(1)}, u32[]{:S(2)}, u32[]{:S(2)}) async-start(bf16[64,4,128]{2,1,0:T(4,128)(2,1)} %bitcast.16), calls=%async_computation.3 | async-start | bytes 131072 | tf_op jit(solution)/shard_map/all_to_all | solution.py:355
  99.0 1.3 collective-permute-start.6
  100.3 13.9 %all-to-all-done.3 = bf16[64,4,128]{2,1,0:T(4,128)(2,1)S(1)} async-done(((bf16[64,4,128]{2,1,0:T(4,128)(2,1)}), bf16[64,4,128]{2,1,0:T(4,128)(2,1)S(1)}, u32[]{:S(2)}, u32[]{:S(2)}) %all-to-all-start.3) | async-done | bytes 65568 | tf_op jit(solution)/shard_map/all_to_all | solution.py:355
  114.2 4.4 %collective-permute-start.8 = (bf16[256,128]{1,0:T(8,128)(2,1)S(1)}, bf16[256,128]{1,0:T(8,128)(2,1)S(1)}, u32[]{:S(2)}, u32[]{:S(2)}) collective-permute-start(bf16[256,128]{1,0:T(8,128)(2,1)S(1)} %bitcast.36), channel_id=1, source_target_pairs={{0,384},{64,448},{128,0},{192,64},{256,128},{320,192},{384,256},{4... | collective-permute-start | bytes 196616 | tf_op jit(solution)/shard_map/ppermute | solution.py:351
  118.6 0.0 collective-permute-done.6.refs_2_
  118.7 0.0 collective-permute-done.5.refs_0_
  118.7 0.0 copy-start.3
  118.7 1.0 copy-done.3
  119.6 4.3 %inside.3 = (f32[128,4096]{1,0:T(8,128)S(1)}, f32[8,4096]{1,0:T(8,128)S(1)}) custom-call(bf16[128,4096]{1,0:T(8,128)(2,1)} %copy-done.3, bf16[128,4096]{1,0:T(8,128)(2,1)} %collective-permute-done.3.refs_7_.refs_1_, bf16[16,4096]{1,0:T(8,128)(2,1)S(1)} %collective-permute-done.6.refs_2_, bf16[512,128]{1,0:T(8,128)(2,1)S(1)} %bitcast.23, ...), custom_call_target="tpu_custom_call" | custom-call | flops 2147483648 | bytes 8388608 | tf_op jit(solution)/shard_map/inside/pallas_call | solution.py:318
  124.0 0.0 collective-permute-done.8.refs_3_
  124.0 5.3 %last.1 = bf16[128,4096]{1,0:T(8,128)(2,1)} custom-call(bf16[128,4096]{1,0:T(8,128)(2,1)} %copy-done.3, f32[128,4096]{1,0:T(8,128)S(1)} %get-tuple-element.24.refs_1_, f32[8,4096]{1,0:T(8,128)S(1)} %get-tuple-element.25.refs_2_, bf16[256,128]{1,0:T(8,128)(2,1)S(1)} %collective-permute-done.8.refs_3_, f32[7,4096]{1,0:T(8,128)S(1)} %collective-permute-done.4.refs_8_.refs_4_, ...), custom_call_target="tpu_custom_call" | custom-call | bytes 8388608 | tf_op jit(solution)/shard_map/last/pallas_call | solution.py:318
  (1 shorter events, 0.0 us)
Async XLA Ops:
  0.0 24.1 %copy-start.4 = (f32[1,2,7,4096]{3,1,2,0:T(2,128)S(1)}, f32[1,2,7,4096]{3,1,2,0:T(2,128)}, u32[]{:S(2)}) copy-start(f32[1,2,7,4096]{3,1,2,0:T(2,128)} %param.9) | copy-start | bytes 688132
  0.0 47.8 %copy-start = (bf16[1240,256]{1,0:T(8,128)(2,1)S(1)}, bf16[1240,256]{1,0:T(8,128)(2,1)}, u32[]{:S(2)}) copy-start(bf16[1240,256]{1,0:T(8,128)(2,1)} %constant.5.clone.refs_4_.refs_6_.refs_5_) | copy-start | bytes 1904644
  3.4 36.4 %all-to-all-start = ((bf16[64,8,128]{2,1,0:T(8,128)(2,1)}), bf16[64,8,128]{2,1,0:T(8,128)(2,1)S(1)}, u32[]{:S(2)}, u32[]{:S(2)}) async-start(bf16[64,8,128]{2,1,0:T(8,128)(2,1)} %bitcast.6), calls=%async_computation | async-start | bytes 262144 | tf_op jit(solution)/shard_map/all_to_all | solution.py:355
  22.2 2.1 %collective-permute-start.1 = (f32[32,64]{1,0:T(8,128)S(1)}, f32[32,64]{1,0:T(8,128)S(1)}, u32[]{:S(2)}, u32[]{:S(2)}) collective-permute-start(f32[32,64]{1,0:T(8,128)S(1)} %get-tuple-element.20), channel_id=1, source_target_pairs={{0,448},{64,0},{128,64},{192,128},{256,192},{320,256},{384,320},{4... | collective-permute-start | bytes 24584 | tf_op jit(solution)/shard_map/ppermute | solution.py:351
  22.2 41.6 %collective-permute-start.3 = (bf16[128,4096]{1,0:T(8,128)(2,1)}, bf16[128,4096]{1,0:T(8,128)(2,1)}, u32[]{:S(2)}, u32[]{:S(2)}) collective-permute-start(bf16[128,4096]{1,0:T(8,128)(2,1)} %get-tuple-element.21), channel_id=1, source_target_pairs={{0,448},{64,0},{128,64},{192,128},{256,192},{320,256},{384,320},{4... | collective-permute-start | bytes 3145736 | tf_op jit(solution)/shard_map/ppermute | solution.py:351
  22.8 41.0 %collective-permute-start.2 = (bf16[128,4096]{1,0:T(8,128)(2,1)}, bf16[128,4096]{1,0:T(8,128)(2,1)}, u32[]{:S(2)}, u32[]{:S(2)}) collective-permute-start(bf16[128,4096]{1,0:T(8,128)(2,1)} %get-tuple-element.21), channel_id=1, source_target_pairs={{0,64},{64,128},{128,192},{192,256},{256,320},{320,384},{384,448},... | collective-permute-start | bytes 3145736 | tf_op jit(solution)/shard_map/ppermute | solution.py:351
  22.9 24.3 %collective-permute-start = (bf16[16,4096]{1,0:T(8,128)(2,1)S(1)}, bf16[16,4096]{1,0:T(8,128)(2,1)S(1)}, u32[]{:S(2)}, u32[]{:S(2)}) collective-permute-start(bf16[16,4096]{1,0:T(8,128)(2,1)S(1)} %get-tuple-element.16), channel_id=1, source_target_pairs={{1,0},{2,1},{3,2},{4,3},{5,4},{6,5},{7,6},{8,7},{9,8},{10,9},{11,1... | collective-permute-start | bytes 393224 | tf_op jit(solution)/shard_map/ppermute | solution.py:374
  42.5 21.4 %all-to-all-start.1 = ((bf16[64,8,128]{2,1,0:T(8,128)(2,1)}), bf16[64,8,128]{2,1,0:T(8,128)(2,1)S(1)}, u32[]{:S(2)}, u32[]{:S(2)}) async-start(bf16[64,8,128]{2,1,0:T(8,128)(2,1)} %bitcast.10), calls=%async_computation.1 | async-start | bytes 262144 | tf_op jit(solution)/shard_map/all_to_all | solution.py:355
  47.1 5.9 %collective-permute-start.4 = (f32[7,4096]{1,0:T(8,128)S(1)}, f32[7,4096]{1,0:T(8,128)S(1)}, u32[]{:S(2)}, u32[]{:S(2)}) collective-permute-start(f32[7,4096]{1,0:T(8,128)S(1)} %slice_bitcast_fusion), channel_id=1, source_target_pairs={{0,448},{64,0},{128,64},{192,128},{256,192},{320,256},{384,320},{4... | collective-permute-start | bytes 344072 | tf_op jit(solution)/shard_map/ppermute | solution.py:351
  47.1 0.6 copy-start.1
  47.8 0.9 copy-start.2
  69.9 48.8 %collective-permute-start.5 = (bf16[128,4096]{1,0:T(8,128)(2,1)}, bf16[128,4096]{1,0:T(8,128)(2,1)S(1)}, u32[]{:S(2)}, u32[]{:S(2)}) collective-permute-start(bf16[128,4096]{1,0:T(8,128)(2,1)} %get-tuple-element.22), channel_id=1, source_target_pairs={{0,384},{64,448},{128,0},{192,64},{256,128},{320,192},{384,256},{4... | collective-permute-start | bytes 3145736 | tf_op jit(solution)/shard_map/ppermute | solution.py:351
  72.3 20.2 %all-to-all-start.2 = ((bf16[64,4,128]{2,1,0:T(4,128)(2,1)}), bf16[64,4,128]{2,1,0:T(4,128)(2,1)S(1)}, u32[]{:S(2)}, u32[]{:S(2)}) async-start(bf16[64,4,128]{2,1,0:T(4,128)(2,1)} %bitcast.14), calls=%async_computation.2 | async-start | bytes 131072 | tf_op jit(solution)/shard_map/all_to_all | solution.py:355
  77.3 3.2 %collective-permute-start.7 = (f32[32,64]{1,0:T(8,128)S(1)}, f32[32,64]{1,0:T(8,128)S(1)}, u32[]{:S(2)}, u32[]{:S(2)}) collective-permute-start(f32[32,64]{1,0:T(8,128)S(1)} %get-tuple-element.20), channel_id=1, source_target_pairs={{0,64},{64,128},{128,192},{192,256},{256,320},{320,384},{384,448},... | collective-permute-start | bytes 24584 | tf_op jit(solution)/shard_map/ppermute | solution.py:351
  94.4 19.8 %all-to-all-start.3 = ((bf16[64,4,128]{2,1,0:T(4,128)(2,1)}), bf16[64,4,128]{2,1,0:T(4,128)(2,1)S(1)}, u32[]{:S(2)}, u32[]{:S(2)}) async-start(bf16[64,4,128]{2,1,0:T(4,128)(2,1)} %bitcast.16), calls=%async_computation.3 | async-start | bytes 131072 | tf_op jit(solution)/shard_map/all_to_all | solution.py:355
  99.0 19.7 %collective-permute-start.6 = (bf16[16,4096]{1,0:T(8,128)(2,1)S(1)}, bf16[16,4096]{1,0:T(8,128)(2,1)S(1)}, u32[]{:S(2)}, u32[]{:S(2)}) collective-permute-start(bf16[16,4096]{1,0:T(8,128)(2,1)S(1)} %get-tuple-element.23), channel_id=1, source_target_pairs={{1,384},{2,385},{3,386},{4,387},{5,388},{6,389},{7,390},{8,391},{9... | collective-permute-start | bytes 393224 | tf_op jit(solution)/shard_map/ppermute | solution.py:397
  114.2 9.8 %collective-permute-start.8 = (bf16[256,128]{1,0:T(8,128)(2,1)S(1)}, bf16[256,128]{1,0:T(8,128)(2,1)S(1)}, u32[]{:S(2)}, u32[]{:S(2)}) collective-permute-start(bf16[256,128]{1,0:T(8,128)(2,1)S(1)} %bitcast.36), channel_id=1, source_target_pairs={{0,384},{64,448},{128,0},{192,64},{256,128},{320,192},{384,256},{4... | collective-permute-start | bytes 196616 | tf_op jit(solution)/shard_map/ppermute | solution.py:351
  118.7 1.0 copy-start.3

commit v3 on v2

--- a/solution.py
+++ b/solution.py
@@ -292,6 +292,10 @@
         copy.wait()
 
 
+def order_kernel(nodes_ref, rim_ref, out_ref):
+    out_ref[...] = nodes_ref[...]
+
+
 def last_kernel(
     g_far, local_ref, rim_ref, nodes_ref, short_ref, matrix_ref, out_far, g_near, out_near, g_sem, out_sem
 ):
@@ -400,11 +404,20 @@
     (back,) = call(
         scan_last_kernel, "scan", [got, params_early], [short_pay_shape], fixed=(source, gaps, rows)
     )
-    nodes = around(across(back), -2)
+    nodes = across(back)
     local, rim = call(
         inside_kernel, "inside", [g, gates_late, halo, taps, matrices], local_shapes,
         flops=2 * NODES * rows * 2 * rows * channels,
     )
+    nodes = pl.pallas_call(
+        order_kernel,
+        in_specs=[pl.BlockSpec(memory_space=pltpu.VMEM), anywhere],
+        out_specs=pl.BlockSpec(memory_space=pltpu.VMEM),
+        out_shape=short_pay_shape,
+        compiler_params=PARAMS,
+        name="order",
+    )(nodes, rim)
+    nodes = around(nodes, -2)
     (g,) = call(
         last_kernel, "last", [g, local, rim, nodes, short_late, matrices], [row_shape],
         specs={0: anywhere}, out_specs={0: anywhere}, scratch=near * 2 + sems * 2,

time: 130 us -> 129 us (level)
  the two profiles are of different devices: /device:TPU:2 before, /device:TPU:8 now
where the time goes in v3:
time: 129 us
  starting transfers between devices  53.5 us (41%)
  waiting for transfers between devices  45.5 us (35%)
  Pallas kernels  27.8 us (22%)
  local copies, waits for them, and re-layouts  1.71 us (1%)
    all_to_all x4, starting transfers between devices, across(): lax.all_to_all(blocks, 'seq', split_axis=0, concat_axis=0, tiled=True)  38.1 us
    all_to_all x4, waiting for transfers between devices, across(): lax.all_to_all(blocks, 'seq', split_axis=0, concat_axis=0, tiled=True)  36.9 us
    pallas_call x7, Pallas kernels, call(): pl.pallas_call(lambda *refs: kernel(*fixed, *refs), **{'scratch_shapes':...  27.8 us
    ppermute x7, starting transfers between devices, around(): lax.ppermute(x, 'segment', [(i, (i + distance) % segments) for i in range...  10.3 us
    ppermute x7, waiting for transfers between devices, around(): lax.ppermute(x, 'segment', [(i, (i + distance) % segments) for i in range...  8.61 us
    ppermute x1, starting transfers between devices, on_device(): halo = lax.ppermute(halo, ('segment', 'seq'), moves)  2.74 us
  transfers between devices with their start and end apart: 13, of which 6 were waited for; matrix products, arithmetic and copies ran while one was open for 0% of the time, Pallas kernels for 10%

profile of v3, /device:TPU:8, one launch (start us, length us, event | category | flops | bytes accessed | tf_op | source)
XLA Modules:
  0.0 128.9 jit_solution(4050480231145127682)
XLA Ops:
  0.0 0.0 copy-start.3
  0.0 0.0 copy-start
  0.0 3.4 %first.1 = (bf16[512,128]{1,0:T(8,128)(2,1)}, bf16[16,4096]{1,0:T(8,128)(2,1)S(1)}, f32[32,64]{1,0:T(8,128)S(1)}, bf16[128,4096]{1,0:T(8,128)(2,1)}) custom-call(bf16[128,4096]{1,0:T(8,128)(2,1)} %bitcast.28, bf16[2,128,4096]{2,1,0:T(8,128)(2,1)} %bitcast.31, f32[2,16,64]{2,1,0:T(8,128)} %bitcast.33, f32[2,16,64]{2,1,0:T(8,128)} %bitcast.35, ...), custom_call_target="tpu_custom_call" | custom-call | bytes 8388608 | tf_op jit(solution)/shard_map/first/pallas_call | solution.py:322
  3.5 18.7 %all-to-all-start = ((bf16[64,8,128]{2,1,0:T(8,128)(2,1)}), bf16[64,8,128]{2,1,0:T(8,128)(2,1)S(1)}, u32[]{:S(2)}, u32[]{:S(2)}) async-start(bf16[64,8,128]{2,1,0:T(8,128)(2,1)} %bitcast.6), calls=%async_computation | async-start | bytes 262144 | tf_op jit(solution)/shard_map/all_to_all | solution.py:359
  22.2 1.6 %collective-permute-start.1 = (f32[32,64]{1,0:T(8,128)S(1)}, f32[32,64]{1,0:T(8,128)S(1)}, u32[]{:S(2)}, u32[]{:S(2)}) collective-permute-start(f32[32,64]{1,0:T(8,128)S(1)} %get-tuple-element.20), channel_id=1, source_target_pairs={{0,448},{64,0},{128,64},{192,128},{256,192},{320,256},{384,320},{4... | collective-permute-start | bytes 24584 | tf_op jit(solution)/shard_map/ppermute | solution.py:355
  23.8 1.2 collective-permute-start.3
  25.1 0.0 collective-permute-start.2
  25.1 2.4 %collective-permute-start = (bf16[16,4096]{1,0:T(8,128)(2,1)S(1)}, bf16[16,4096]{1,0:T(8,128)(2,1)S(1)}, u32[]{:S(2)}, u32[]{:S(2)}) collective-permute-start(bf16[16,4096]{1,0:T(8,128)(2,1)S(1)} %get-tuple-element.16), channel_id=1, source_target_pairs={{1,0},{2,1},{3,2},{4,3},{5,4},{6,5},{7,6},{8,7},{9,8},{10,9},{11,1... | collective-permute-start | bytes 393224 | tf_op jit(solution)/shard_map/ppermute | solution.py:378
  27.4 0.0 copy-done.3
  27.4 0.1 copy.12
  27.6 0.0 collective-permute-done.1.refs_3_
  27.6 11.2 %all-to-all-done = bf16[64,8,128]{2,1,0:T(8,128)(2,1)S(1)} async-done(((bf16[64,8,128]{2,1,0:T(8,128)(2,1)}), bf16[64,8,128]{2,1,0:T(8,128)(2,1)S(1)}, u32[]{:S(2)}, u32[]{:S(2)}) %all-to-all-start) | async-done | bytes 131104 | tf_op jit(solution)/shard_map/all_to_all | solution.py:359
  38.8 2.6 %scan.2 = bf16[512,128]{1,0:T(8,128)(2,1)} custom-call(bf16[512,128]{1,0:T(8,128)(2,1)S(1)} %bitcast.24, f32[2,16,64]{2,1,0:T(8,128)} %bitcast.34, f32[2,16,64]{2,1,0:T(8,128)} %bitcast.36, f32[32,64]{1,0:T(8,128)S(1)} %collective-permute-done.1.refs_3_), custom_call_target="tpu_custom_call" | custom-call | bytes 8388608 | tf_op jit(solution)/shard_map/scan/pallas_call | solution.py:322
  41.4 5.6 %all-to-all-start.1 = ((bf16[64,8,128]{2,1,0:T(8,128)(2,1)}), bf16[64,8,128]{2,1,0:T(8,128)(2,1)S(1)}, u32[]{:S(2)}, u32[]{:S(2)}) async-start(bf16[64,8,128]{2,1,0:T(8,128)(2,1)} %bitcast.10), calls=%async_computation.1 | async-start | bytes 262144 | tf_op jit(solution)/shard_map/all_to_all | solution.py:359
  47.0 0.8 collective-permute-start.4
  47.8 0.0 collective-permute-done.refs_2_
  47.8 0.0 copy-start.1
  47.8 0.6 copy-done.1
  48.4 0.0 copy-done
  48.4 0.0 copy-start.2
  48.4 0.9 copy-done.2
  49.3 4.3 %inside.2 = (f32[128,4096]{1,0:T(8,128)S(1)}, f32[8,4096]{1,0:T(8,128)S(1)}) custom-call(bf16[128,4096]{1,0:T(8,128)(2,1)} %bitcast.29, bf16[2,128,4096]{2,1,0:T(8,128)(2,1)} %bitcast.32, bf16[16,4096]{1,0:T(8,128)(2,1)S(1)} %copy-done.2, bf16[512,128]{1,0:T(8,128)(2,1)S(1)} %bitcast.25, bf16[1240,256]{1,0:T(8,128)(2,1)S(1)} %copy-done), custom_call_target="tpu_custom_call" | custom-call | flops 2147483648 | bytes 8388608 | tf_op jit(solution)/shard_map/inside/pallas_call | solution.py:322
  53.7 0.0 collective-permute-done.4.refs_8_.refs_4_
  53.7 8.9 %all-to-all-done.1 = bf16[64,8,128]{2,1,0:T(8,128)(2,1)S(1)} async-done(((bf16[64,8,128]{2,1,0:T(8,128)(2,1)}), bf16[64,8,128]{2,1,0:T(8,128)(2,1)S(1)}, u32[]{:S(2)}, u32[]{:S(2)}) %all-to-all-start.1) | async-done | bytes 131104 | tf_op jit(solution)/shard_map/all_to_all | solution.py:359
  62.6 0.0 collective-permute-done.3.refs_7_.refs_1_
  62.6 0.0 collective-permute-done.2.refs_5_
  62.6 6.0 %turn.1 = (bf16[128,4096]{1,0:T(8,128)(2,1)}, bf16[256,128]{1,0:T(8,128)(2,1)}, bf16[16,4096]{1,0:T(8,128)(2,1)S(1)}) custom-call(bf16[128,4096]{1,0:T(8,128)(2,1)} %bitcast.30, f32[128,4096]{1,0:T(8,128)S(1)} %get-tuple-element.18.refs_1_, f32[8,4096]{1,0:T(8,128)S(1)} %get-tuple-element.19.refs_2_, bf16[512,128]{1,0:T(8,128)(2,1)S(1)} %bitcast.22, ...), custom_call_target="tpu_custom_call" | custom-call | bytes 8388608 | tf_op jit(solution)/shard_map/turn/pallas_call | solution.py:322
  68.6 4.7 %collective-permute-start.5 = (bf16[128,4096]{1,0:T(8,128)(2,1)}, bf16[128,4096]{1,0:T(8,128)(2,1)}, u32[]{:S(2)}, u32[]{:S(2)}) collective-permute-start(bf16[128,4096]{1,0:T(8,128)(2,1)} %get-tuple-element.22), channel_id=1, source_target_pairs={{0,384},{64,448},{128,0},{192,64},{256,128},{320,192},{384,256},{4... | collective-permute-start | bytes 3145736 | tf_op jit(solution)/shard_map/ppermute | solution.py:355
  73.3 5.7 %all-to-all-start.2 = ((bf16[64,4,128]{2,1,0:T(4,128)(2,1)}), bf16[64,4,128]{2,1,0:T(4,128)(2,1)S(1)}, u32[]{:S(2)}, u32[]{:S(2)}) async-start(bf16[64,4,128]{2,1,0:T(4,128)(2,1)} %bitcast.14), calls=%async_computation.2 | async-start | bytes 131072 | tf_op jit(solution)/shard_map/all_to_all | solution.py:359
  79.0 2.7 %collective-permute-start.6 = (bf16[16,4096]{1,0:T(8,128)(2,1)S(1)}, bf16[16,4096]{1,0:T(8,128)(2,1)S(1)}, u32[]{:S(2)}, u32[]{:S(2)}) collective-permute-start(bf16[16,4096]{1,0:T(8,128)(2,1)S(1)} %get-tuple-element.23), channel_id=1, source_target_pairs={{1,384},{2,385},{3,386},{4,387},{5,388},{6,389},{7,390},{8,391},{9... | collective-permute-start | bytes 393224 | tf_op jit(solution)/shard_map/ppermute | solution.py:401
  81.8 0.0 collective-permute-start.7
  81.8 4.4 %collective-permute-done.7.refs_1_ = f32[32,64]{1,0:T(8,128)S(1)} collective-permute-done((f32[32,64]{1,0:T(8,128)S(1)}, f32[32,64]{1,0:T(8,128)S(1)}, u32[]{:S(2)}, u32[]{:S(2)}) %collective-permute-start.7) | collective-permute-done | bytes 8224 | tf_op jit(solution)/shard_map/ppermute | solution.py:355
  86.2 7.1 %all-to-all-done.2 = bf16[64,4,128]{2,1,0:T(4,128)(2,1)S(1)} async-done(((bf16[64,4,128]{2,1,0:T(4,128)(2,1)}), bf16[64,4,128]{2,1,0:T(4,128)(2,1)S(1)}, u32[]{:S(2)}, u32[]{:S(2)}) %all-to-all-start.2) | async-done | bytes 65568 | tf_op jit(solution)/shard_map/all_to_all | solution.py:359
  93.3 1.8 %scan.3 = bf16[256,128]{1,0:T(8,128)(2,1)} custom-call(bf16[256,128]{1,0:T(8,128)(2,1)S(1)} %bitcast.26, f32[32,64]{1,0:T(8,128)S(1)} %collective-permute-done.7.refs_1_), custom_call_target="tpu_custom_call" | custom-call | bytes 8388608 | tf_op jit(solution)/shard_map/scan/pallas_call | solution.py:322
  95.0 8.1 %all-to-all-start.3 = ((bf16[64,4,128]{2,1,0:T(4,128)(2,1)}), bf16[64,4,128]{2,1,0:T(4,128)(2,1)S(1)}, u32[]{:S(2)}, u32[]{:S(2)}) async-start(bf16[64,4,128]{2,1,0:T(4,128)(2,1)} %bitcast.16), calls=%async_computation.3 | async-start | bytes 131072 | tf_op jit(solution)/shard_map/all_to_all | solution.py:359
  103.2 0.0 collective-permute-done.6.refs_2_
  103.2 0.0 collective-permute-done.5.refs_0_
  103.2 4.4 %inside.3 = (f32[128,4096]{1,0:T(8,128)S(1)}, f32[8,4096]{1,0:T(8,128)S(1)}) custom-call(bf16[128,4096]{1,0:T(8,128)(2,1)} %collective-permute-done.5.refs_0_, bf16[128,4096]{1,0:T(8,128)(2,1)} %collective-permute-done.3.refs_7_.refs_1_, bf16[16,4096]{1,0:T(8,128)(2,1)S(1)} %collective-permute-done.6.refs_2_, bf16[512,128]{1,0:T(8,128)(2,1)S(1)} %bitcast.23, ...), custom_call_target="tpu_custom_call" | custom-call | flops 2147483648 | bytes 8388608 | tf_op jit(solution)/shard_map/inside/pallas_call | solution.py:322
  107.5 9.8 %all-to-all-done.3 = bf16[64,4,128]{2,1,0:T(4,128)(2,1)S(1)} async-done(((bf16[64,4,128]{2,1,0:T(4,128)(2,1)}), bf16[64,4,128]{2,1,0:T(4,128)(2,1)S(1)}, u32[]{:S(2)}, u32[]{:S(2)}) %all-to-all-start.3) | async-done | bytes 65568 | tf_op jit(solution)/shard_map/all_to_all | solution.py:359
  117.3 1.9 %collective-permute-start.8 = (bf16[256,128]{1,0:T(8,128)(2,1)S(1)}, bf16[256,128]{1,0:T(8,128)(2,1)S(1)}, u32[]{:S(2)}, u32[]{:S(2)}) collective-permute-start(bf16[256,128]{1,0:T(8,128)(2,1)S(1)} %order.1), channel_id=1, source_target_pairs={{0,384},{64,448},{128,0},{192,64},{256,128},{320,192},{384,256},{4... | collective-permute-start | bytes 196616 | tf_op jit(solution)/shard_map/ppermute | solution.py:355
  119.2 4.2 %collective-permute-done.8.refs_3_ = bf16[256,128]{1,0:T(8,128)(2,1)S(1)} collective-permute-done((bf16[256,128]{1,0:T(8,128)(2,1)S(1)}, bf16[256,128]{1,0:T(8,128)(2,1)S(1)}, u32[]{:S(2)}, u32[]{:S(2)}) %collective-permute-start.8) | collective-permute-done | bytes 65568 | tf_op jit(solution)/shard_map/ppermute | solution.py:355
  123.5 5.3 %last.1 = bf16[128,4096]{1,0:T(8,128)(2,1)} custom-call(bf16[128,4096]{1,0:T(8,128)(2,1)} %collective-permute-done.5.refs_0_, f32[128,4096]{1,0:T(8,128)S(1)} %get-tuple-element.24.refs_1_, f32[8,4096]{1,0:T(8,128)S(1)} %get-tuple-element.25.rim_ref.refs_2_, bf16[256,128]{1,0:T(8,128)(2,1)S(1)} %collective-permute-done.8.refs_3_, ...), custom_call_target="tpu_custom_call" | custom-call | bytes 8388608 | tf_op jit(solution)/shard_map/last/pallas_call | solution.py:322
  (2 shorter events, 0.0 us)
Async XLA Ops:
  0.0 27.4 %copy-start.3 = (f32[1,2,7,4096]{3,1,2,0:T(2,128)S(1)}, f32[1,2,7,4096]{3,1,2,0:T(2,128)}, u32[]{:S(2)}) copy-start(f32[1,2,7,4096]{3,1,2,0:T(2,128)} %param.9) | copy-start | bytes 688132
  0.0 48.4 %copy-start = (bf16[1240,256]{1,0:T(8,128)(2,1)S(1)}, bf16[1240,256]{1,0:T(8,128)(2,1)}, u32[]{:S(2)}) copy-start(bf16[1240,256]{1,0:T(8,128)(2,1)} %constant.5.clone.refs_4_.refs_6_.refs_5_) | copy-start | bytes 1904644
  3.5 35.3 %all-to-all-start = ((bf16[64,8,128]{2,1,0:T(8,128)(2,1)}), bf16[64,8,128]{2,1,0:T(8,128)(2,1)S(1)}, u32[]{:S(2)}, u32[]{:S(2)}) async-start(bf16[64,8,128]{2,1,0:T(8,128)(2,1)} %bitcast.6), calls=%async_computation | async-start | bytes 262144 | tf_op jit(solution)/shard_map/all_to_all | solution.py:359
  22.2 5.4 %collective-permute-start.1 = (f32[32,64]{1,0:T(8,128)S(1)}, f32[32,64]{1,0:T(8,128)S(1)}, u32[]{:S(2)}, u32[]{:S(2)}) collective-permute-start(f32[32,64]{1,0:T(8,128)S(1)} %get-tuple-element.20), channel_id=1, source_target_pairs={{0,448},{64,0},{128,64},{192,128},{256,192},{320,256},{384,320},{4... | collective-permute-start | bytes 24584 | tf_op jit(solution)/shard_map/ppermute | solution.py:355
  23.8 38.7 %collective-permute-start.3 = (bf16[128,4096]{1,0:T(8,128)(2,1)}, bf16[128,4096]{1,0:T(8,128)(2,1)}, u32[]{:S(2)}, u32[]{:S(2)}) collective-permute-start(bf16[128,4096]{1,0:T(8,128)(2,1)} %get-tuple-element.21), channel_id=1, source_target_pairs={{0,448},{64,0},{128,64},{192,128},{256,192},{320,256},{384,320},{4... | collective-permute-start | bytes 3145736 | tf_op jit(solution)/shard_map/ppermute | solution.py:355
  25.1 37.5 %collective-permute-start.2 = (bf16[128,4096]{1,0:T(8,128)(2,1)}, bf16[128,4096]{1,0:T(8,128)(2,1)}, u32[]{:S(2)}, u32[]{:S(2)}) collective-permute-start(bf16[128,4096]{1,0:T(8,128)(2,1)} %get-tuple-element.21), channel_id=1, source_target_pairs={{0,64},{64,128},{128,192},{192,256},{256,320},{320,384},{384,448},... | collective-permute-start | bytes 3145736 | tf_op jit(solution)/shard_map/ppermute | solution.py:355
  25.1 22.7 %collective-permute-start = (bf16[16,4096]{1,0:T(8,128)(2,1)S(1)}, bf16[16,4096]{1,0:T(8,128)(2,1)S(1)}, u32[]{:S(2)}, u32[]{:S(2)}) collective-permute-start(bf16[16,4096]{1,0:T(8,128)(2,1)S(1)} %get-tuple-element.16), channel_id=1, source_target_pairs={{1,0},{2,1},{3,2},{4,3},{5,4},{6,5},{7,6},{8,7},{9,8},{10,9},{11,1... | collective-permute-start | bytes 393224 | tf_op jit(solution)/shard_map/ppermute | solution.py:378
  41.4 21.2 %all-to-all-start.1 = ((bf16[64,8,128]{2,1,0:T(8,128)(2,1)}), bf16[64,8,128]{2,1,0:T(8,128)(2,1)S(1)}, u32[]{:S(2)}, u32[]{:S(2)}) async-start(bf16[64,8,128]{2,1,0:T(8,128)(2,1)} %bitcast.10), calls=%async_computation.1 | async-start | bytes 262144 | tf_op jit(solution)/shard_map/all_to_all | solution.py:359
  47.0 6.7 %collective-permute-start.4 = (f32[7,4096]{1,0:T(8,128)S(1)}, f32[7,4096]{1,0:T(8,128)S(1)}, u32[]{:S(2)}, u32[]{:S(2)}) collective-permute-start(f32[7,4096]{1,0:T(8,128)S(1)} %slice_bitcast_fusion), channel_id=1, source_target_pairs={{0,448},{64,0},{128,64},{192,128},{256,192},{320,256},{384,320},{4... | collective-permute-start | bytes 344072 | tf_op jit(solution)/shard_map/ppermute | solution.py:355
  47.8 0.6 copy-start.1
  48.4 0.9 copy-start.2
  68.6 34.6 %collective-permute-start.5 = (bf16[128,4096]{1,0:T(8,128)(2,1)}, bf16[128,4096]{1,0:T(8,128)(2,1)}, u32[]{:S(2)}, u32[]{:S(2)}) collective-permute-start(bf16[128,4096]{1,0:T(8,128)(2,1)} %get-tuple-element.22), channel_id=1, source_target_pairs={{0,384},{64,448},{128,0},{192,64},{256,128},{320,192},{384,256},{4... | collective-permute-start | bytes 3145736 | tf_op jit(solution)/shard_map/ppermute | solution.py:355
  73.3 20.0 %all-to-all-start.2 = ((bf16[64,4,128]{2,1,0:T(4,128)(2,1)}), bf16[64,4,128]{2,1,0:T(4,128)(2,1)S(1)}, u32[]{:S(2)}, u32[]{:S(2)}) async-start(bf16[64,4,128]{2,1,0:T(4,128)(2,1)} %bitcast.14), calls=%async_computation.2 | async-start | bytes 131072 | tf_op jit(solution)/shard_map/all_to_all | solution.py:359
  79.0 24.1 %collective-permute-start.6 = (bf16[16,4096]{1,0:T(8,128)(2,1)S(1)}, bf16[16,4096]{1,0:T(8,128)(2,1)S(1)}, u32[]{:S(2)}, u32[]{:S(2)}) collective-permute-start(bf16[16,4096]{1,0:T(8,128)(2,1)S(1)} %get-tuple-element.23), channel_id=1, source_target_pairs={{1,384},{2,385},{3,386},{4,387},{5,388},{6,389},{7,390},{8,391},{9... | collective-permute-start | bytes 393224 | tf_op jit(solution)/shard_map/ppermute | solution.py:401
  81.8 4.4 %collective-permute-start.7 = (f32[32,64]{1,0:T(8,128)S(1)}, f32[32,64]{1,0:T(8,128)S(1)}, u32[]{:S(2)}, u32[]{:S(2)}) collective-permute-start(f32[32,64]{1,0:T(8,128)S(1)} %get-tuple-element.20), channel_id=1, source_target_pairs={{0,64},{64,128},{128,192},{192,256},{256,320},{320,384},{384,448},... | collective-permute-start | bytes 24584 | tf_op jit(solution)/shard_map/ppermute | solution.py:355
  95.0 22.3 %all-to-all-start.3 = ((bf16[64,4,128]{2,1,0:T(4,128)(2,1)}), bf16[64,4,128]{2,1,0:T(4,128)(2,1)S(1)}, u32[]{:S(2)}, u32[]{:S(2)}) async-start(bf16[64,4,128]{2,1,0:T(4,128)(2,1)} %bitcast.16), calls=%async_computation.3 | async-start | bytes 131072 | tf_op jit(solution)/shard_map/all_to_all | solution.py:359
  117.3 6.1 %collective-permute-start.8 = (bf16[256,128]{1,0:T(8,128)(2,1)S(1)}, bf16[256,128]{1,0:T(8,128)(2,1)S(1)}, u32[]{:S(2)}, u32[]{:S(2)}) collective-permute-start(bf16[256,128]{1,0:T(8,128)(2,1)S(1)} %order.1), channel_id=1, source_target_pairs={{0,384},{64,448},{128,0},{192,64},{256,128},{320,192},{384,256},{4... | collective-permute-start | bytes 196616 | tf_op jit(solution)/shard_map/ppermute | solution.py:355

commit v4 on v3

--- a/solution.py
+++ b/solution.py
@@ -11,7 +11,7 @@
 NODES = 8
 HALF = NODES // 2
 RATE_LOW, RATE_HIGH = 3.66e-5, 0.0333334
-TILE = 512
+TILE = 1024
 VMEM_MIB = 44
 BF = jnp.bfloat16
 F32 = jnp.float32

time: 129 us -> 127 us (0.984)
  Pallas kernels: 27.8 us -> 25.4 us
    pallas_call x7, Pallas kernels: 27.8 us -> 25.4 us  [call(): pl.pallas_call(lambda *refs: kernel(*fixed, *refs), **{'scratch_shapes':...]
where the time goes in v4:
time: 127 us
  starting transfers between devices  53.5 us (42%)
  waiting for transfers between devices  45.8 us (36%)
  Pallas kernels  25.4 us (20%)
  local copies, waits for them, and re-layouts  1.71 us (1%)
    all_to_all x4, starting transfers between devices, across(): lax.all_to_all(blocks, 'seq', split_axis=0, concat_axis=0, tiled=True)  38.1 us
    all_to_all x4, waiting for transfers between devices, across(): lax.all_to_all(blocks, 'seq', split_axis=0, concat_axis=0, tiled=True)  37.2 us
    pallas_call x7, Pallas kernels, call(): pl.pallas_call(lambda *refs: kernel(*fixed, *refs), **{'scratch_shapes':...  25.4 us
    ppermute x7, starting transfers between devices, around(): lax.ppermute(x, 'segment', [(i, (i + distance) % segments) for i in range...  10.3 us
    ppermute x7, waiting for transfers between devices, around(): lax.ppermute(x, 'segment', [(i, (i + distance) % segments) for i in range...  8.61 us
    ppermute x1, starting transfers between devices, on_device(): halo = lax.ppermute(halo, ('segment', 'seq'), moves)  2.74 us
  transfers between devices with their start and end apart: 13, of which 6 were waited for; matrix products, arithmetic and copies ran while one was open for 0% of the time, Pallas kernels for 10%

profile of v4, /device:TPU:8, one launch (start us, length us, event | category | flops | bytes accessed | tf_op | source)
XLA Modules:
  0.0 126.8 jit_solution(2666657754045421789)
XLA Ops:
  0.0 0.0 copy-start.3
  0.0 0.0 copy-start
  0.0 3.4 %first.1 = (bf16[512,128]{1,0:T(8,128)(2,1)}, bf16[16,4096]{1,0:T(8,128)(2,1)S(1)}, f32[32,64]{1,0:T(8,128)S(1)}, bf16[128,4096]{1,0:T(8,128)(2,1)}) custom-call(bf16[128,4096]{1,0:T(8,128)(2,1)} %bitcast.28, bf16[2,128,4096]{2,1,0:T(8,128)(2,1)} %bitcast.31, f32[2,16,64]{2,1,0:T(8,128)} %bitcast.33, f32[2,16,64]{2,1,0:T(8,128)} %bitcast.35, ...), custom_call_target="tpu_custom_call" | custom-call | bytes 8388608 | tf_op jit(solution)/shard_map/first/pallas_call | solution.py:322
  3.4 18.7 %all-to-all-start = ((bf16[64,8,128]{2,1,0:T(8,128)(2,1)}), bf16[64,8,128]{2,1,0:T(8,128)(2,1)S(1)}, u32[]{:S(2)}, u32[]{:S(2)}) async-start(bf16[64,8,128]{2,1,0:T(8,128)(2,1)} %bitcast.6), calls=%async_computation | async-start | bytes 262144 | tf_op jit(solution)/shard_map/all_to_all | solution.py:359
  22.2 1.6 %collective-permute-start.1 = (f32[32,64]{1,0:T(8,128)S(1)}, f32[32,64]{1,0:T(8,128)S(1)}, u32[]{:S(2)}, u32[]{:S(2)}) collective-permute-start(f32[32,64]{1,0:T(8,128)S(1)} %get-tuple-element.20), channel_id=1, source_target_pairs={{0,448},{64,0},{128,64},{192,128},{256,192},{320,256},{384,320},{4... | collective-permute-start | bytes 24584 | tf_op jit(solution)/shard_map/ppermute | solution.py:355
  23.8 1.2 collective-permute-start.3
  25.0 0.0 collective-permute-start.2
  25.1 2.4 %collective-permute-start = (bf16[16,4096]{1,0:T(8,128)(2,1)S(1)}, bf16[16,4096]{1,0:T(8,128)(2,1)S(1)}, u32[]{:S(2)}, u32[]{:S(2)}) collective-permute-start(bf16[16,4096]{1,0:T(8,128)(2,1)S(1)} %get-tuple-element.16), channel_id=1, source_target_pairs={{1,0},{2,1},{3,2},{4,3},{5,4},{6,5},{7,6},{8,7},{9,8},{10,9},{11,1... | collective-permute-start | bytes 393224 | tf_op jit(solution)/shard_map/ppermute | solution.py:378
  27.4 0.0 copy-done.3
  27.4 0.1 copy.12
  27.6 0.0 collective-permute-done.1.refs_3_
  27.6 11.2 %all-to-all-done = bf16[64,8,128]{2,1,0:T(8,128)(2,1)S(1)} async-done(((bf16[64,8,128]{2,1,0:T(8,128)(2,1)}), bf16[64,8,128]{2,1,0:T(8,128)(2,1)S(1)}, u32[]{:S(2)}, u32[]{:S(2)}) %all-to-all-start) | async-done | bytes 131104 | tf_op jit(solution)/shard_map/all_to_all | solution.py:359
  38.7 2.6 %scan.2 = bf16[512,128]{1,0:T(8,128)(2,1)} custom-call(bf16[512,128]{1,0:T(8,128)(2,1)S(1)} %bitcast.24, f32[2,16,64]{2,1,0:T(8,128)} %bitcast.34, f32[2,16,64]{2,1,0:T(8,128)} %bitcast.36, f32[32,64]{1,0:T(8,128)S(1)} %collective-permute-done.1.refs_3_), custom_call_target="tpu_custom_call" | custom-call | bytes 8388608 | tf_op jit(solution)/shard_map/scan/pallas_call | solution.py:322
  41.3 5.6 %all-to-all-start.1 = ((bf16[64,8,128]{2,1,0:T(8,128)(2,1)}), bf16[64,8,128]{2,1,0:T(8,128)(2,1)S(1)}, u32[]{:S(2)}, u32[]{:S(2)}) async-start(bf16[64,8,128]{2,1,0:T(8,128)(2,1)} %bitcast.10), calls=%async_computation.1 | async-start | bytes 262144 | tf_op jit(solution)/shard_map/all_to_all | solution.py:359
  47.0 0.8 collective-permute-start.4
  47.7 0.0 collective-permute-done.refs_2_
  47.7 0.0 copy-start.1
  47.7 0.6 copy-done.1
  48.4 0.0 copy-done
  48.4 0.0 copy-start.2
  48.4 0.9 copy-done.2
  49.3 4.2 %inside.2 = (f32[128,4096]{1,0:T(8,128)S(1)}, f32[8,4096]{1,0:T(8,128)S(1)}) custom-call(bf16[128,4096]{1,0:T(8,128)(2,1)} %bitcast.29, bf16[2,128,4096]{2,1,0:T(8,128)(2,1)} %bitcast.32, bf16[16,4096]{1,0:T(8,128)(2,1)S(1)} %copy-done.2, bf16[512,128]{1,0:T(8,128)(2,1)S(1)} %bitcast.25, bf16[1240,256]{1,0:T(8,128)(2,1)S(1)} %copy-done), custom_call_target="tpu_custom_call" | custom-call | flops 2147483648 | bytes 8388608 | tf_op jit(solution)/shard_map/inside/pallas_call | solution.py:322
  53.5 0.0 collective-permute-done.4.refs_8_.refs_4_
  53.5 9.0 %all-to-all-done.1 = bf16[64,8,128]{2,1,0:T(8,128)(2,1)S(1)} async-done(((bf16[64,8,128]{2,1,0:T(8,128)(2,1)}), bf16[64,8,128]{2,1,0:T(8,128)(2,1)S(1)}, u32[]{:S(2)}, u32[]{:S(2)}) %all-to-all-start.1) | async-done | bytes 131104 | tf_op jit(solution)/shard_map/all_to_all | solution.py:359
  62.5 0.0 collective-permute-done.3.refs_7_.refs_1_
  62.5 0.0 collective-permute-done.2.refs_5_
  62.5 4.9 %turn.1 = (bf16[128,4096]{1,0:T(8,128)(2,1)}, bf16[256,128]{1,0:T(8,128)(2,1)}, bf16[16,4096]{1,0:T(8,128)(2,1)S(1)}) custom-call(bf16[128,4096]{1,0:T(8,128)(2,1)} %bitcast.30, f32[128,4096]{1,0:T(8,128)S(1)} %get-tuple-element.18.refs_1_, f32[8,4096]{1,0:T(8,128)S(1)} %get-tuple-element.19.refs_2_, bf16[512,128]{1,0:T(8,128)(2,1)S(1)} %bitcast.22, ...), custom_call_target="tpu_custom_call" | custom-call | bytes 8388608 | tf_op jit(solution)/shard_map/turn/pallas_call | solution.py:322
  67.5 4.7 %collective-permute-start.5 = (bf16[128,4096]{1,0:T(8,128)(2,1)}, bf16[128,4096]{1,0:T(8,128)(2,1)}, u32[]{:S(2)}, u32[]{:S(2)}) collective-permute-start(bf16[128,4096]{1,0:T(8,128)(2,1)} %get-tuple-element.22), channel_id=1, source_target_pairs={{0,384},{64,448},{128,0},{192,64},{256,128},{320,192},{384,256},{4... | collective-permute-start | bytes 3145736 | tf_op jit(solution)/shard_map/ppermute | solution.py:355
  72.2 5.7 %all-to-all-start.2 = ((bf16[64,4,128]{2,1,0:T(4,128)(2,1)}), bf16[64,4,128]{2,1,0:T(4,128)(2,1)S(1)}, u32[]{:S(2)}, u32[]{:S(2)}) async-start(bf16[64,4,128]{2,1,0:T(4,128)(2,1)} %bitcast.14), calls=%async_computation.2 | async-start | bytes 131072 | tf_op jit(solution)/shard_map/all_to_all | solution.py:359
  77.9 2.7 %collective-permute-start.6 = (bf16[16,4096]{1,0:T(8,128)(2,1)S(1)}, bf16[16,4096]{1,0:T(8,128)(2,1)S(1)}, u32[]{:S(2)}, u32[]{:S(2)}) collective-permute-start(bf16[16,4096]{1,0:T(8,128)(2,1)S(1)} %get-tuple-element.23), channel_id=1, source_target_pairs={{1,384},{2,385},{3,386},{4,387},{5,388},{6,389},{7,390},{8,391},{9... | collective-permute-start | bytes 393224 | tf_op jit(solution)/shard_map/ppermute | solution.py:401
  80.6 0.0 collective-permute-start.7
  80.7 4.4 %collective-permute-done.7.refs_1_ = f32[32,64]{1,0:T(8,128)S(1)} collective-permute-done((f32[32,64]{1,0:T(8,128)S(1)}, f32[32,64]{1,0:T(8,128)S(1)}, u32[]{:S(2)}, u32[]{:S(2)}) %collective-permute-start.7) | collective-permute-done | bytes 8224 | tf_op jit(solution)/shard_map/ppermute | solution.py:355
  85.0 7.1 %all-to-all-done.2 = bf16[64,4,128]{2,1,0:T(4,128)(2,1)S(1)} async-done(((bf16[64,4,128]{2,1,0:T(4,128)(2,1)}), bf16[64,4,128]{2,1,0:T(4,128)(2,1)S(1)}, u32[]{:S(2)}, u32[]{:S(2)}) %all-to-all-start.2) | async-done | bytes 65568 | tf_op jit(solution)/shard_map/all_to_all | solution.py:359
  92.1 1.8 %scan.3 = bf16[256,128]{1,0:T(8,128)(2,1)} custom-call(bf16[256,128]{1,0:T(8,128)(2,1)S(1)} %bitcast.26, f32[32,64]{1,0:T(8,128)S(1)} %collective-permute-done.7.refs_1_), custom_call_target="tpu_custom_call" | custom-call | bytes 8388608 | tf_op jit(solution)/shard_map/scan/pallas_call | solution.py:322
  93.9 8.1 %all-to-all-start.3 = ((bf16[64,4,128]{2,1,0:T(4,128)(2,1)}), bf16[64,4,128]{2,1,0:T(4,128)(2,1)S(1)}, u32[]{:S(2)}, u32[]{:S(2)}) async-start(bf16[64,4,128]{2,1,0:T(4,128)(2,1)} %bitcast.16), calls=%async_computation.3 | async-start | bytes 131072 | tf_op jit(solution)/shard_map/all_to_all | solution.py:359
  102.0 0.0 collective-permute-done.6.refs_2_
  102.0 0.0 collective-permute-done.5.refs_0_
  102.1 4.2 %inside.3 = (f32[128,4096]{1,0:T(8,128)S(1)}, f32[8,4096]{1,0:T(8,128)S(1)}) custom-call(bf16[128,4096]{1,0:T(8,128)(2,1)} %collective-permute-done.5.refs_0_, bf16[128,4096]{1,0:T(8,128)(2,1)} %collective-permute-done.3.refs_7_.refs_1_, bf16[16,4096]{1,0:T(8,128)(2,1)S(1)} %collective-permute-done.6.refs_2_, bf16[512,128]{1,0:T(8,128)(2,1)S(1)} %bitcast.23, ...), custom_call_target="tpu_custom_call" | custom-call | flops 2147483648 | bytes 8388608 | tf_op jit(solution)/shard_map/inside/pallas_call | solution.py:322
  106.3 9.9 %all-to-all-done.3 = bf16[64,4,128]{2,1,0:T(4,128)(2,1)S(1)} async-done(((bf16[64,4,128]{2,1,0:T(4,128)(2,1)}), bf16[64,4,128]{2,1,0:T(4,128)(2,1)S(1)}, u32[]{:S(2)}, u32[]{:S(2)}) %all-to-all-start.3) | async-done | bytes 65568 | tf_op jit(solution)/shard_map/all_to_all | solution.py:359
  116.2 1.9 %collective-permute-start.8 = (bf16[256,128]{1,0:T(8,128)(2,1)S(1)}, bf16[256,128]{1,0:T(8,128)(2,1)S(1)}, u32[]{:S(2)}, u32[]{:S(2)}) collective-permute-start(bf16[256,128]{1,0:T(8,128)(2,1)S(1)} %order.1), channel_id=1, source_target_pairs={{0,384},{64,448},{128,0},{192,64},{256,128},{320,192},{384,256},{4... | collective-permute-start | bytes 196616 | tf_op jit(solution)/shard_map/ppermute | solution.py:355
  118.1 4.2 %collective-permute-done.8.refs_3_ = bf16[256,128]{1,0:T(8,128)(2,1)S(1)} collective-permute-done((bf16[256,128]{1,0:T(8,128)(2,1)S(1)}, bf16[256,128]{1,0:T(8,128)(2,1)S(1)}, u32[]{:S(2)}, u32[]{:S(2)}) %collective-permute-start.8) | collective-permute-done | bytes 65568 | tf_op jit(solution)/shard_map/ppermute | solution.py:355
  122.3 4.3 %last.1 = bf16[128,4096]{1,0:T(8,128)(2,1)} custom-call(bf16[128,4096]{1,0:T(8,128)(2,1)} %collective-permute-done.5.refs_0_, f32[128,4096]{1,0:T(8,128)S(1)} %get-tuple-element.24.refs_1_, f32[8,4096]{1,0:T(8,128)S(1)} %get-tuple-element.25.rim_ref.refs_2_, bf16[256,128]{1,0:T(8,128)(2,1)S(1)} %collective-permute-done.8.refs_3_, ...), custom_call_target="tpu_custom_call" | custom-call | bytes 8388608 | tf_op jit(solution)/shard_map/last/pallas_call | solution.py:322
  (2 shorter events, 0.0 us)
Async XLA Ops:
  0.0 27.4 %copy-start.3 = (f32[1,2,7,4096]{3,1,2,0:T(2,128)S(1)}, f32[1,2,7,4096]{3,1,2,0:T(2,128)}, u32[]{:S(2)}) copy-start(f32[1,2,7,4096]{3,1,2,0:T(2,128)} %param.9) | copy-start | bytes 688132
  0.0 48.4 %copy-start = (bf16[1240,256]{1,0:T(8,128)(2,1)S(1)}, bf16[1240,256]{1,0:T(8,128)(2,1)}, u32[]{:S(2)}) copy-start(bf16[1240,256]{1,0:T(8,128)(2,1)} %constant.5.clone.refs_4_.refs_6_.refs_5_) | copy-start | bytes 1904644
  3.4 35.3 %all-to-all-start = ((bf16[64,8,128]{2,1,0:T(8,128)(2,1)}), bf16[64,8,128]{2,1,0:T(8,128)(2,1)S(1)}, u32[]{:S(2)}, u32[]{:S(2)}) async-start(bf16[64,8,128]{2,1,0:T(8,128)(2,1)} %bitcast.6), calls=%async_computation | async-start | bytes 262144 | tf_op jit(solution)/shard_map/all_to_all | solution.py:359
  22.2 5.4 %collective-permute-start.1 = (f32[32,64]{1,0:T(8,128)S(1)}, f32[32,64]{1,0:T(8,128)S(1)}, u32[]{:S(2)}, u32[]{:S(2)}) collective-permute-start(f32[32,64]{1,0:T(8,128)S(1)} %get-tuple-element.20), channel_id=1, source_target_pairs={{0,448},{64,0},{128,64},{192,128},{256,192},{320,256},{384,320},{4... | collective-permute-start | bytes 24584 | tf_op jit(solution)/shard_map/ppermute | solution.py:355
  23.8 38.7 %collective-permute-start.3 = (bf16[128,4096]{1,0:T(8,128)(2,1)}, bf16[128,4096]{1,0:T(8,128)(2,1)}, u32[]{:S(2)}, u32[]{:S(2)}) collective-permute-start(bf16[128,4096]{1,0:T(8,128)(2,1)} %get-tuple-element.21), channel_id=1, source_target_pairs={{0,448},{64,0},{128,64},{192,128},{256,192},{320,256},{384,320},{4... | collective-permute-start | bytes 3145736 | tf_op jit(solution)/shard_map/ppermute | solution.py:355
  25.0 37.5 %collective-permute-start.2 = (bf16[128,4096]{1,0:T(8,128)(2,1)}, bf16[128,4096]{1,0:T(8,128)(2,1)}, u32[]{:S(2)}, u32[]{:S(2)}) collective-permute-start(bf16[128,4096]{1,0:T(8,128)(2,1)} %get-tuple-element.21), channel_id=1, source_target_pairs={{0,64},{64,128},{128,192},{192,256},{256,320},{320,384},{384,448},... | collective-permute-start | bytes 3145736 | tf_op jit(solution)/shard_map/ppermute | solution.py:355
  25.1 22.7 %collective-permute-start = (bf16[16,4096]{1,0:T(8,128)(2,1)S(1)}, bf16[16,4096]{1,0:T(8,128)(2,1)S(1)}, u32[]{:S(2)}, u32[]{:S(2)}) collective-permute-start(bf16[16,4096]{1,0:T(8,128)(2,1)S(1)} %get-tuple-element.16), channel_id=1, source_target_pairs={{1,0},{2,1},{3,2},{4,3},{5,4},{6,5},{7,6},{8,7},{9,8},{10,9},{11,1... | collective-permute-start | bytes 393224 | tf_op jit(solution)/shard_map/ppermute | solution.py:378
  41.3 21.2 %all-to-all-start.1 = ((bf16[64,8,128]{2,1,0:T(8,128)(2,1)}), bf16[64,8,128]{2,1,0:T(8,128)(2,1)S(1)}, u32[]{:S(2)}, u32[]{:S(2)}) async-start(bf16[64,8,128]{2,1,0:T(8,128)(2,1)} %bitcast.10), calls=%async_computation.1 | async-start | bytes 262144 | tf_op jit(solution)/shard_map/all_to_all | solution.py:359
  47.0 6.5 %collective-permute-start.4 = (f32[7,4096]{1,0:T(8,128)S(1)}, f32[7,4096]{1,0:T(8,128)S(1)}, u32[]{:S(2)}, u32[]{:S(2)}) collective-permute-start(f32[7,4096]{1,0:T(8,128)S(1)} %slice_bitcast_fusion), channel_id=1, source_target_pairs={{0,448},{64,0},{128,64},{192,128},{256,192},{320,256},{384,320},{4... | collective-permute-start | bytes 344072 | tf_op jit(solution)/shard_map/ppermute | solution.py:355
  47.7 0.6 copy-start.1
  48.4 0.9 copy-start.2
  67.5 34.6 %collective-permute-start.5 = (bf16[128,4096]{1,0:T(8,128)(2,1)}, bf16[128,4096]{1,0:T(8,128)(2,1)}, u32[]{:S(2)}, u32[]{:S(2)}) collective-permute-start(bf16[128,4096]{1,0:T(8,128)(2,1)} %get-tuple-element.22), channel_id=1, source_target_pairs={{0,384},{64,448},{128,0},{192,64},{256,128},{320,192},{384,256},{4... | collective-permute-start | bytes 3145736 | tf_op jit(solution)/shard_map/ppermute | solution.py:355
  72.2 20.0 %all-to-all-start.2 = ((bf16[64,4,128]{2,1,0:T(4,128)(2,1)}), bf16[64,4,128]{2,1,0:T(4,128)(2,1)S(1)}, u32[]{:S(2)}, u32[]{:S(2)}) async-start(bf16[64,4,128]{2,1,0:T(4,128)(2,1)} %bitcast.14), calls=%async_computation.2 | async-start | bytes 131072 | tf_op jit(solution)/shard_map/all_to_all | solution.py:359
  77.9 24.1 %collective-permute-start.6 = (bf16[16,4096]{1,0:T(8,128)(2,1)S(1)}, bf16[16,4096]{1,0:T(8,128)(2,1)S(1)}, u32[]{:S(2)}, u32[]{:S(2)}) collective-permute-start(bf16[16,4096]{1,0:T(8,128)(2,1)S(1)} %get-tuple-element.23), channel_id=1, source_target_pairs={{1,384},{2,385},{3,386},{4,387},{5,388},{6,389},{7,390},{8,391},{9... | collective-permute-start | bytes 393224 | tf_op jit(solution)/shard_map/ppermute | solution.py:401
  80.6 4.4 %collective-permute-start.7 = (f32[32,64]{1,0:T(8,128)S(1)}, f32[32,64]{1,0:T(8,128)S(1)}, u32[]{:S(2)}, u32[]{:S(2)}) collective-permute-start(f32[32,64]{1,0:T(8,128)S(1)} %get-tuple-element.20), channel_id=1, source_target_pairs={{0,64},{64,128},{128,192},{192,256},{256,320},{320,384},{384,448},... | collective-permute-start | bytes 24584 | tf_op jit(solution)/shard_map/ppermute | solution.py:355
  93.9 22.2 %all-to-all-start.3 = ((bf16[64,4,128]{2,1,0:T(4,128)(2,1)}), bf16[64,4,128]{2,1,0:T(4,128)(2,1)S(1)}, u32[]{:S(2)}, u32[]{:S(2)}) async-start(bf16[64,4,128]{2,1,0:T(4,128)(2,1)} %bitcast.16), calls=%async_computation.3 | async-start | bytes 131072 | tf_op jit(solution)/shard_map/all_to_all | solution.py:359
  116.2 6.1 %collective-permute-start.8 = (bf16[256,128]{1,0:T(8,128)(2,1)S(1)}, bf16[256,128]{1,0:T(8,128)(2,1)S(1)}, u32[]{:S(2)}, u32[]{:S(2)}) collective-permute-start(bf16[256,128]{1,0:T(8,128)(2,1)S(1)} %order.1), channel_id=1, source_target_pairs={{0,384},{64,448},{128,0},{192,64},{256,128},{320,192},{384,256},{4... | collective-permute-start | bytes 196616 | tf_op jit(solution)/shard_map/ppermute | solution.py:355

commit v5 on v4

--- a/solution.py
+++ b/solution.py
@@ -11,7 +11,7 @@
 NODES = 8
 HALF = NODES // 2
 RATE_LOW, RATE_HIGH = 3.66e-5, 0.0333334
-TILE = 1024
+TILE = 2048
 VMEM_MIB = 44
 BF = jnp.bfloat16
 F32 = jnp.float32

time: 127 us -> 126 us (level)
  no operation moved by 1% of the time
where the time goes in v5:
time: 126 us
  starting transfers between devices  53.5 us (42%)
  waiting for transfers between devices  46.1 us (37%)
  Pallas kernels  24.2 us (19%)
  local copies, waits for them, and re-layouts  1.71 us (1%)
    all_to_all x4, starting transfers between devices, across(): lax.all_to_all(blocks, 'seq', split_axis=0, concat_axis=0, tiled=True)  38.1 us
    all_to_all x4, waiting for transfers between devices, across(): lax.all_to_all(blocks, 'seq', split_axis=0, concat_axis=0, tiled=True)  37.4 us
    pallas_call x7, Pallas kernels, call(): pl.pallas_call(lambda *refs: kernel(*fixed, *refs), **{'scratch_shapes':...  24.2 us
    ppermute x7, starting transfers between devices, around(): lax.ppermute(x, 'segment', [(i, (i + distance) % segments) for i in range...  10.3 us
    ppermute x7, waiting for transfers between devices, around(): lax.ppermute(x, 'segment', [(i, (i + distance) % segments) for i in range...  8.61 us
    ppermute x1, starting transfers between devices, on_device(): halo = lax.ppermute(halo, ('segment', 'seq'), moves)  2.74 us
  transfers between devices with their start and end apart: 13, of which 6 were waited for; matrix products, arithmetic and copies ran while one was open for 0% of the time, Pallas kernels for 10%

profile of v5, /device:TPU:8, one launch (start us, length us, event | category | flops | bytes accessed | tf_op | source)
XLA Modules:
  0.0 125.7 jit_solution(16121580031387863648)
XLA Ops:
  0.0 0.0 copy-start.3
  0.0 0.0 copy-start
  0.0 3.4 %first.1 = (bf16[512,128]{1,0:T(8,128)(2,1)}, bf16[16,4096]{1,0:T(8,128)(2,1)S(1)}, f32[32,64]{1,0:T(8,128)S(1)}, bf16[128,4096]{1,0:T(8,128)(2,1)}) custom-call(bf16[128,4096]{1,0:T(8,128)(2,1)} %bitcast.28, bf16[2,128,4096]{2,1,0:T(8,128)(2,1)} %bitcast.31, f32[2,16,64]{2,1,0:T(8,128)} %bitcast.33, f32[2,16,64]{2,1,0:T(8,128)} %bitcast.35, ...), custom_call_target="tpu_custom_call" | custom-call | bytes 8388608 | tf_op jit(solution)/shard_map/first/pallas_call | solution.py:322
  3.4 18.7 %all-to-all-start = ((bf16[64,8,128]{2,1,0:T(8,128)(2,1)}), bf16[64,8,128]{2,1,0:T(8,128)(2,1)S(1)}, u32[]{:S(2)}, u32[]{:S(2)}) async-start(bf16[64,8,128]{2,1,0:T(8,128)(2,1)} %bitcast.6), calls=%async_computation | async-start | bytes 262144 | tf_op jit(solution)/shard_map/all_to_all | solution.py:359
  22.2 1.6 %collective-permute-start.1 = (f32[32,64]{1,0:T(8,128)S(1)}, f32[32,64]{1,0:T(8,128)S(1)}, u32[]{:S(2)}, u32[]{:S(2)}) collective-permute-start(f32[32,64]{1,0:T(8,128)S(1)} %get-tuple-element.20), channel_id=1, source_target_pairs={{0,448},{64,0},{128,64},{192,128},{256,192},{320,256},{384,320},{4... | collective-permute-start | bytes 24584 | tf_op jit(solution)/shard_map/ppermute | solution.py:355
  23.8 1.2 collective-permute-start.3
  25.0 0.0 collective-permute-start.2
  25.1 2.4 %collective-permute-start = (bf16[16,4096]{1,0:T(8,128)(2,1)S(1)}, bf16[16,4096]{1,0:T(8,128)(2,1)S(1)}, u32[]{:S(2)}, u32[]{:S(2)}) collective-permute-start(bf16[16,4096]{1,0:T(8,128)(2,1)S(1)} %get-tuple-element.16), channel_id=1, source_target_pairs={{1,0},{2,1},{3,2},{4,3},{5,4},{6,5},{7,6},{8,7},{9,8},{10,9},{11,1... | collective-permute-start | bytes 393224 | tf_op jit(solution)/shard_map/ppermute | solution.py:378
  27.4 0.0 copy-done.3
  27.4 0.1 copy.12
  27.6 0.0 collective-permute-done.1.refs_3_
  27.6 11.2 %all-to-all-done = bf16[64,8,128]{2,1,0:T(8,128)(2,1)S(1)} async-done(((bf16[64,8,128]{2,1,0:T(8,128)(2,1)}), bf16[64,8,128]{2,1,0:T(8,128)(2,1)S(1)}, u32[]{:S(2)}, u32[]{:S(2)}) %all-to-all-start) | async-done | bytes 131104 | tf_op jit(solution)/shard_map/all_to_all | solution.py:359
  38.7 2.6 %scan.2 = bf16[512,128]{1,0:T(8,128)(2,1)} custom-call(bf16[512,128]{1,0:T(8,128)(2,1)S(1)} %bitcast.24, f32[2,16,64]{2,1,0:T(8,128)} %bitcast.34, f32[2,16,64]{2,1,0:T(8,128)} %bitcast.36, f32[32,64]{1,0:T(8,128)S(1)} %collective-permute-done.1.refs_3_), custom_call_target="tpu_custom_call" | custom-call | bytes 8388608 | tf_op jit(solution)/shard_map/scan/pallas_call | solution.py:322
  41.3 5.6 %all-to-all-start.1 = ((bf16[64,8,128]{2,1,0:T(8,128)(2,1)}), bf16[64,8,128]{2,1,0:T(8,128)(2,1)S(1)}, u32[]{:S(2)}, u32[]{:S(2)}) async-start(bf16[64,8,128]{2,1,0:T(8,128)(2,1)} %bitcast.10), calls=%async_computation.1 | async-start | bytes 262144 | tf_op jit(solution)/shard_map/all_to_all | solution.py:359
  47.0 0.8 collective-permute-start.4
  47.7 0.0 collective-permute-done.refs_2_
  47.7 0.0 copy-start.1
  47.7 0.6 copy-done.1
  48.4 0.0 copy-done
  48.4 0.0 copy-start.2
  48.4 0.9 copy-done.2
  49.3 4.1 %inside.2 = (f32[128,4096]{1,0:T(8,128)S(1)}, f32[8,4096]{1,0:T(8,128)S(1)}) custom-call(bf16[128,4096]{1,0:T(8,128)(2,1)} %bitcast.29, bf16[2,128,4096]{2,1,0:T(8,128)(2,1)} %bitcast.32, bf16[16,4096]{1,0:T(8,128)(2,1)S(1)} %copy-done.2, bf16[512,128]{1,0:T(8,128)(2,1)S(1)} %bitcast.25, bf16[1240,256]{1,0:T(8,128)(2,1)S(1)} %copy-done), custom_call_target="tpu_custom_call" | custom-call | flops 2147483648 | bytes 8388608 | tf_op jit(solution)/shard_map/inside/pallas_call | solution.py:322
  53.4 0.0 collective-permute-done.4.refs_8_.refs_4_
  53.4 9.1 %all-to-all-done.1 = bf16[64,8,128]{2,1,0:T(8,128)(2,1)S(1)} async-done(((bf16[64,8,128]{2,1,0:T(8,128)(2,1)}), bf16[64,8,128]{2,1,0:T(8,128)(2,1)S(1)}, u32[]{:S(2)}, u32[]{:S(2)}) %all-to-all-start.1) | async-done | bytes 131104 | tf_op jit(solution)/shard_map/all_to_all | solution.py:359
  62.5 0.0 collective-permute-done.3.refs_7_.refs_1_
  62.5 0.0 collective-permute-done.2.refs_5_
  62.5 4.4 %turn.1 = (bf16[128,4096]{1,0:T(8,128)(2,1)}, bf16[256,128]{1,0:T(8,128)(2,1)}, bf16[16,4096]{1,0:T(8,128)(2,1)S(1)}) custom-call(bf16[128,4096]{1,0:T(8,128)(2,1)} %bitcast.30, f32[128,4096]{1,0:T(8,128)S(1)} %get-tuple-element.18.refs_1_, f32[8,4096]{1,0:T(8,128)S(1)} %get-tuple-element.19.refs_2_, bf16[512,128]{1,0:T(8,128)(2,1)S(1)} %bitcast.22, ...), custom_call_target="tpu_custom_call" | custom-call | bytes 8388608 | tf_op jit(solution)/shard_map/turn/pallas_call | solution.py:322
  66.9 4.7 %collective-permute-start.5 = (bf16[128,4096]{1,0:T(8,128)(2,1)}, bf16[128,4096]{1,0:T(8,128)(2,1)}, u32[]{:S(2)}, u32[]{:S(2)}) collective-permute-start(bf16[128,4096]{1,0:T(8,128)(2,1)} %get-tuple-element.22), channel_id=1, source_target_pairs={{0,384},{64,448},{128,0},{192,64},{256,128},{320,192},{384,256},{4... | collective-permute-start | bytes 3145736 | tf_op jit(solution)/shard_map/ppermute | solution.py:355
  71.6 5.7 %all-to-all-start.2 = ((bf16[64,4,128]{2,1,0:T(4,128)(2,1)}), bf16[64,4,128]{2,1,0:T(4,128)(2,1)S(1)}, u32[]{:S(2)}, u32[]{:S(2)}) async-start(bf16[64,4,128]{2,1,0:T(4,128)(2,1)} %bitcast.14), calls=%async_computation.2 | async-start | bytes 131072 | tf_op jit(solution)/shard_map/all_to_all | solution.py:359
  77.3 2.7 %collective-permute-start.6 = (bf16[16,4096]{1,0:T(8,128)(2,1)S(1)}, bf16[16,4096]{1,0:T(8,128)(2,1)S(1)}, u32[]{:S(2)}, u32[]{:S(2)}) collective-permute-start(bf16[16,4096]{1,0:T(8,128)(2,1)S(1)} %get-tuple-element.23), channel_id=1, source_target_pairs={{1,384},{2,385},{3,386},{4,387},{5,388},{6,389},{7,390},{8,391},{9... | collective-permute-start | bytes 393224 | tf_op jit(solution)/shard_map/ppermute | solution.py:401
  80.1 0.0 collective-permute-start.7
  80.1 4.4 %collective-permute-done.7.refs_1_ = f32[32,64]{1,0:T(8,128)S(1)} collective-permute-done((f32[32,64]{1,0:T(8,128)S(1)}, f32[32,64]{1,0:T(8,128)S(1)}, u32[]{:S(2)}, u32[]{:S(2)}) %collective-permute-start.7) | collective-permute-done | bytes 8224 | tf_op jit(solution)/shard_map/ppermute | solution.py:355
  84.5 7.1 %all-to-all-done.2 = bf16[64,4,128]{2,1,0:T(4,128)(2,1)S(1)} async-done(((bf16[64,4,128]{2,1,0:T(4,128)(2,1)}), bf16[64,4,128]{2,1,0:T(4,128)(2,1)S(1)}, u32[]{:S(2)}, u32[]{:S(2)}) %all-to-all-start.2) | async-done | bytes 65568 | tf_op jit(solution)/shard_map/all_to_all | solution.py:359
  91.6 1.8 %scan.3 = bf16[256,128]{1,0:T(8,128)(2,1)} custom-call(bf16[256,128]{1,0:T(8,128)(2,1)S(1)} %bitcast.26, f32[32,64]{1,0:T(8,128)S(1)} %collective-permute-done.7.refs_1_), custom_call_target="tpu_custom_call" | custom-call | bytes 8388608 | tf_op jit(solution)/shard_map/scan/pallas_call | solution.py:322
  93.4 8.1 %all-to-all-start.3 = ((bf16[64,4,128]{2,1,0:T(4,128)(2,1)}), bf16[64,4,128]{2,1,0:T(4,128)(2,1)S(1)}, u32[]{:S(2)}, u32[]{:S(2)}) async-start(bf16[64,4,128]{2,1,0:T(4,128)(2,1)} %bitcast.16), calls=%async_computation.3 | async-start | bytes 131072 | tf_op jit(solution)/shard_map/all_to_all | solution.py:359
  101.5 0.0 collective-permute-done.6.refs_2_
  101.5 0.0 collective-permute-done.5.refs_0_
  101.5 4.1 %inside.3 = (f32[128,4096]{1,0:T(8,128)S(1)}, f32[8,4096]{1,0:T(8,128)S(1)}) custom-call(bf16[128,4096]{1,0:T(8,128)(2,1)} %collective-permute-done.5.refs_0_, bf16[128,4096]{1,0:T(8,128)(2,1)} %collective-permute-done.3.refs_7_.refs_1_, bf16[16,4096]{1,0:T(8,128)(2,1)S(1)} %collective-permute-done.6.refs_2_, bf16[512,128]{1,0:T(8,128)(2,1)S(1)} %bitcast.23, ...), custom_call_target="tpu_custom_call" | custom-call | flops 2147483648 | bytes 8388608 | tf_op jit(solution)/shard_map/inside/pallas_call | solution.py:322
  105.6 10.0 %all-to-all-done.3 = bf16[64,4,128]{2,1,0:T(4,128)(2,1)S(1)} async-done(((bf16[64,4,128]{2,1,0:T(4,128)(2,1)}), bf16[64,4,128]{2,1,0:T(4,128)(2,1)S(1)}, u32[]{:S(2)}, u32[]{:S(2)}) %all-to-all-start.3) | async-done | bytes 65568 | tf_op jit(solution)/shard_map/all_to_all | solution.py:359
  115.6 1.9 %collective-permute-start.8 = (bf16[256,128]{1,0:T(8,128)(2,1)S(1)}, bf16[256,128]{1,0:T(8,128)(2,1)S(1)}, u32[]{:S(2)}, u32[]{:S(2)}) collective-permute-start(bf16[256,128]{1,0:T(8,128)(2,1)S(1)} %order.1), channel_id=1, source_target_pairs={{0,384},{64,448},{128,0},{192,64},{256,128},{320,192},{384,256},{4... | collective-permute-start | bytes 196616 | tf_op jit(solution)/shard_map/ppermute | solution.py:355
  117.5 4.2 %collective-permute-done.8.refs_3_ = bf16[256,128]{1,0:T(8,128)(2,1)S(1)} collective-permute-done((bf16[256,128]{1,0:T(8,128)(2,1)S(1)}, bf16[256,128]{1,0:T(8,128)(2,1)S(1)}, u32[]{:S(2)}, u32[]{:S(2)}) %collective-permute-start.8) | collective-permute-done | bytes 65568 | tf_op jit(solution)/shard_map/ppermute | solution.py:355
  121.8 3.8 %last.1 = bf16[128,4096]{1,0:T(8,128)(2,1)} custom-call(bf16[128,4096]{1,0:T(8,128)(2,1)} %collective-permute-done.5.refs_0_, f32[128,4096]{1,0:T(8,128)S(1)} %get-tuple-element.24.refs_1_, f32[8,4096]{1,0:T(8,128)S(1)} %get-tuple-element.25.rim_ref.refs_2_, bf16[256,128]{1,0:T(8,128)(2,1)S(1)} %collective-permute-done.8.refs_3_, ...), custom_call_target="tpu_custom_call" | custom-call | bytes 8388608 | tf_op jit(solution)/shard_map/last/pallas_call | solution.py:322
  (2 shorter events, 0.0 us)
Async XLA Ops:
  0.0 27.4 %copy-start.3 = (f32[1,2,7,4096]{3,1,2,0:T(2,128)S(1)}, f32[1,2,7,4096]{3,1,2,0:T(2,128)}, u32[]{:S(2)}) copy-start(f32[1,2,7,4096]{3,1,2,0:T(2,128)} %param.9) | copy-start | bytes 688132
  0.0 48.4 %copy-start = (bf16[1240,256]{1,0:T(8,128)(2,1)S(1)}, bf16[1240,256]{1,0:T(8,128)(2,1)}, u32[]{:S(2)}) copy-start(bf16[1240,256]{1,0:T(8,128)(2,1)} %constant.5.clone.refs_4_.refs_6_.refs_5_) | copy-start | bytes 1904644
  3.4 35.3 %all-to-all-start = ((bf16[64,8,128]{2,1,0:T(8,128)(2,1)}), bf16[64,8,128]{2,1,0:T(8,128)(2,1)S(1)}, u32[]{:S(2)}, u32[]{:S(2)}) async-start(bf16[64,8,128]{2,1,0:T(8,128)(2,1)} %bitcast.6), calls=%async_computation | async-start | bytes 262144 | tf_op jit(solution)/shard_map/all_to_all | solution.py:359
  22.2 5.4 %collective-permute-start.1 = (f32[32,64]{1,0:T(8,128)S(1)}, f32[32,64]{1,0:T(8,128)S(1)}, u32[]{:S(2)}, u32[]{:S(2)}) collective-permute-start(f32[32,64]{1,0:T(8,128)S(1)} %get-tuple-element.20), channel_id=1, source_target_pairs={{0,448},{64,0},{128,64},{192,128},{256,192},{320,256},{384,320},{4... | collective-permute-start | bytes 24584 | tf_op jit(solution)/shard_map/ppermute | solution.py:355
  23.8 38.7 %collective-permute-start.3 = (bf16[128,4096]{1,0:T(8,128)(2,1)}, bf16[128,4096]{1,0:T(8,128)(2,1)}, u32[]{:S(2)}, u32[]{:S(2)}) collective-permute-start(bf16[128,4096]{1,0:T(8,128)(2,1)} %get-tuple-element.21), channel_id=1, source_target_pairs={{0,448},{64,0},{128,64},{192,128},{256,192},{320,256},{384,320},{4... | collective-permute-start | bytes 3145736 | tf_op jit(solution)/shard_map/ppermute | solution.py:355
  25.0 37.5 %collective-permute-start.2 = (bf16[128,4096]{1,0:T(8,128)(2,1)}, bf16[128,4096]{1,0:T(8,128)(2,1)}, u32[]{:S(2)}, u32[]{:S(2)}) collective-permute-start(bf16[128,4096]{1,0:T(8,128)(2,1)} %get-tuple-element.21), channel_id=1, source_target_pairs={{0,64},{64,128},{128,192},{192,256},{256,320},{320,384},{384,448},... | collective-permute-start | bytes 3145736 | tf_op jit(solution)/shard_map/ppermute | solution.py:355
  25.1 22.7 %collective-permute-start = (bf16[16,4096]{1,0:T(8,128)(2,1)S(1)}, bf16[16,4096]{1,0:T(8,128)(2,1)S(1)}, u32[]{:S(2)}, u32[]{:S(2)}) collective-permute-start(bf16[16,4096]{1,0:T(8,128)(2,1)S(1)} %get-tuple-element.16), channel_id=1, source_target_pairs={{1,0},{2,1},{3,2},{4,3},{5,4},{6,5},{7,6},{8,7},{9,8},{10,9},{11,1... | collective-permute-start | bytes 393224 | tf_op jit(solution)/shard_map/ppermute | solution.py:378
  41.3 21.2 %all-to-all-start.1 = ((bf16[64,8,128]{2,1,0:T(8,128)(2,1)}), bf16[64,8,128]{2,1,0:T(8,128)(2,1)S(1)}, u32[]{:S(2)}, u32[]{:S(2)}) async-start(bf16[64,8,128]{2,1,0:T(8,128)(2,1)} %bitcast.10), calls=%async_computation.1 | async-start | bytes 262144 | tf_op jit(solution)/shard_map/all_to_all | solution.py:359
  47.0 6.4 %collective-permute-start.4 = (f32[7,4096]{1,0:T(8,128)S(1)}, f32[7,4096]{1,0:T(8,128)S(1)}, u32[]{:S(2)}, u32[]{:S(2)}) collective-permute-start(f32[7,4096]{1,0:T(8,128)S(1)} %slice_bitcast_fusion), channel_id=1, source_target_pairs={{0,448},{64,0},{128,64},{192,128},{256,192},{320,256},{384,320},{4... | collective-permute-start | bytes 344072 | tf_op jit(solution)/shard_map/ppermute | solution.py:355
  47.7 0.6 copy-start.1
  48.4 0.9 copy-start.2
  66.9 34.6 %collective-permute-start.5 = (bf16[128,4096]{1,0:T(8,128)(2,1)}, bf16[128,4096]{1,0:T(8,128)(2,1)}, u32[]{:S(2)}, u32[]{:S(2)}) collective-permute-start(bf16[128,4096]{1,0:T(8,128)(2,1)} %get-tuple-element.22), channel_id=1, source_target_pairs={{0,384},{64,448},{128,0},{192,64},{256,128},{320,192},{384,256},{4... | collective-permute-start | bytes 3145736 | tf_op jit(solution)/shard_map/ppermute | solution.py:355
  71.6 20.0 %all-to-all-start.2 = ((bf16[64,4,128]{2,1,0:T(4,128)(2,1)}), bf16[64,4,128]{2,1,0:T(4,128)(2,1)S(1)}, u32[]{:S(2)}, u32[]{:S(2)}) async-start(bf16[64,4,128]{2,1,0:T(4,128)(2,1)} %bitcast.14), calls=%async_computation.2 | async-start | bytes 131072 | tf_op jit(solution)/shard_map/all_to_all | solution.py:359
  77.3 24.1 %collective-permute-start.6 = (bf16[16,4096]{1,0:T(8,128)(2,1)S(1)}, bf16[16,4096]{1,0:T(8,128)(2,1)S(1)}, u32[]{:S(2)}, u32[]{:S(2)}) collective-permute-start(bf16[16,4096]{1,0:T(8,128)(2,1)S(1)} %get-tuple-element.23), channel_id=1, source_target_pairs={{1,384},{2,385},{3,386},{4,387},{5,388},{6,389},{7,390},{8,391},{9... | collective-permute-start | bytes 393224 | tf_op jit(solution)/shard_map/ppermute | solution.py:401
  80.1 4.4 %collective-permute-start.7 = (f32[32,64]{1,0:T(8,128)S(1)}, f32[32,64]{1,0:T(8,128)S(1)}, u32[]{:S(2)}, u32[]{:S(2)}) collective-permute-start(f32[32,64]{1,0:T(8,128)S(1)} %get-tuple-element.20), channel_id=1, source_target_pairs={{0,64},{64,128},{128,192},{192,256},{256,320},{320,384},{384,448},... | collective-permute-start | bytes 24584 | tf_op jit(solution)/shard_map/ppermute | solution.py:355
  93.4 22.2 %all-to-all-start.3 = ((bf16[64,4,128]{2,1,0:T(4,128)(2,1)}), bf16[64,4,128]{2,1,0:T(4,128)(2,1)S(1)}, u32[]{:S(2)}, u32[]{:S(2)}) async-start(bf16[64,4,128]{2,1,0:T(4,128)(2,1)} %bitcast.16), calls=%async_computation.3 | async-start | bytes 131072 | tf_op jit(solution)/shard_map/all_to_all | solution.py:359
  115.6 6.1 %collective-permute-start.8 = (bf16[256,128]{1,0:T(8,128)(2,1)S(1)}, bf16[256,128]{1,0:T(8,128)(2,1)S(1)}, u32[]{:S(2)}, u32[]{:S(2)}) collective-permute-start(bf16[256,128]{1,0:T(8,128)(2,1)S(1)} %order.1), channel_id=1, source_target_pairs={{0,384},{64,448},{128,0},{192,64},{256,128},{320,192},{384,256},{4... | collective-permute-start | bytes 196616 | tf_op jit(solution)/shard_map/ppermute | solution.py:355
